TPU v7x, 768 devices: a whole 4x8x12 slice. The times are simulated.
768 devices in a mesh: atm: 96 (over z, x, core), ocn: 8 (over y).
Axes of the slice: x: 4, y: 8, z: 12, core: 2. Of those that a mesh axis runs over, the one named last changes fastest.
Arguments:
- atm_fields: bfloat16 [64, 196608], P(None, ('atm', 'ocn')), may hold values from -6 to 6
- ocn_fields: bfloat16 [64, 294912], P(None, ('atm', 'ocn')), may hold values from -6 to 6
- transfer_scale: float32 [64], replicated, may hold values from 0.5 to 2
- atmosphere_slots: int32 [768, 7, 64], P(('atm', 'ocn')), may hold values from -1 to 255, as said below
- ocn_slots: int32 [768, 8, 96], P(('atm', 'ocn')), may hold values from 0 to 383
- xc_ocean: int32 [768, 2, 448], P(('atm', 'ocn')), may hold values from -1 to 767, as said below
- xc_area: bfloat16 [768, 448], P(('atm', 'ocn')), may hold values from 0.19921875 to 1
- xc_theta: bfloat16 [768, 448], P(('atm', 'ocn')), may hold values from 0.099609375 to 0.8984375
Outputs:
- atm_flux: float32 [64, 196608], P(None, ('atm', 'ocn'))
- ocn_flux: float32 [64, 294912], P(None, ('atm', 'ocn'))
Inputs may be any that keep to these rules, and one draw needn't show every extreme that they name: `atmosphere_slots`: entry [a2 * 8 + o, k, c] is live (not -1) exactly where xc_ocean[a * 8 + o, 0, k * 64 + c] is, with a = (a2 + k - 3) mod 96; live entries of one block and row come first; each owner receives all 64 slots from its own block (k = 3). `xc_ocean`: both rows are -1 exactly in empty slots, and neither is -1 in live ones.
All inputs are finite; a program needn't handle non-finite values.
Results may differ from a plain program's by a relative error of at most 0.0054.
Values may be sent and summed in bfloat16 or wider, within the bound.
No kernel may reach another device: no remote copies, remote signals or barrier semaphores. Data moves between devices by JAX's collectives and lax.ppermute only.
A program may use at most 32 MiB of HBM per device.

v0:
```python
import jax
import jax.numpy as jnp
from jax import lax
from jax.sharding import PartitionSpec as P

RADIUS = 3
SLOT_CAPACITY = 64
ITERS = 3
SOURCE_BLOCKS = 7


def passed_along(block, axis, distance):
    devices = range(lax.axis_size(axis))
    route = [((i - distance) % len(devices), i) for i in devices]
    return lax.ppermute(block, axis, route)


def surface_flux(air, sea, scale, area):
    a = air.astype(jnp.float32)
    s = sea.astype(jnp.float32)
    du = a[..., 1, :] - s[..., 1, :]
    dv = a[..., 2, :] - s[..., 2, :]
    speed = jnp.sqrt(du * du + dv * dv + 0.25)
    contrast = a[..., 0, :] - s[..., 0, :]
    coeff = jnp.ones_like(speed)
    for step in range(ITERS):
        coeff = 1.5 - 0.8 * jnp.tanh(0.3 * contrast * coeff / (speed * speed))
    return area * (scale[:, None] * (coeff * speed)[..., None, :] * (a - s))


def select_cols(table, picker):
    return lax.dot_general(
        table, picker, (((1,), (1,)), ((), ())), preferred_element_type=jnp.float32
    )


def exact_dot(left, right):
    return jnp.dot(left, right, precision=lax.Precision.HIGHEST, preferred_element_type=jnp.float32)


def on_device(
    atm_fields, ocn_fields, transfer_scale, atmosphere_slots, ocn_slots, xc_ocean, xc_area, xc_theta
):
    atm_cells = atm_fields.shape[1]
    ocn_cells = ocn_fields.shape[1]
    atmosphere_index = atmosphere_slots.reshape(-1)
    atm_live = atmosphere_index >= 0
    atm_picker = atmosphere_index[:, None] == jnp.arange(atm_cells, dtype=jnp.int32)[None, :]
    outgoing = select_cols(atm_fields, atm_picker.astype(jnp.bfloat16)).astype(jnp.bfloat16)
    received = []
    for row in range(SOURCE_BLOCKS):
        portion = outgoing[:, row * SLOT_CAPACITY : (row + 1) * SLOT_CAPACITY]
        if row == RADIUS:
            received.append(portion)
        else:
            received.append(passed_along(portion, "atm", row - RADIUS))
    air_slots = jnp.concatenate(received, axis=1)
    sea_index = ocn_slots.reshape(-1)
    ocean_picker = sea_index[:, None] == jnp.arange(ocn_cells, dtype=jnp.int32)[None, :]
    sending = select_cols(ocn_fields, ocean_picker.astype(jnp.bfloat16)).astype(jnp.bfloat16)
    sea_entries = lax.all_to_all(sending, "ocn", split_axis=1, concat_axis=1, tiled=True)
    first_owner = xc_ocean[0, 0]
    second_owner = xc_ocean[0, 1]
    live_mask = first_owner >= 0
    theta = xc_theta[0].astype(jnp.float32)
    area = xc_area[0]
    entry_ids = jnp.arange(sea_entries.shape[1], dtype=jnp.int32)[:, None]
    pick_one = (entry_ids == first_owner[None, :]).astype(jnp.bfloat16)
    pick_two = (entry_ids == second_owner[None, :]).astype(jnp.bfloat16)
    first_vals = jnp.dot(sea_entries, pick_one, preferred_element_type=jnp.float32)
    second_vals = jnp.dot(sea_entries, pick_two, preferred_element_type=jnp.float32)
    sea_slots = (theta[None, :] * first_vals + (1.0 - theta)[None, :] * second_vals).astype(
        jnp.bfloat16
    )
    flux = surface_flux(air_slots, sea_slots, transfer_scale, area.astype(jnp.float32)[None, :])
    weighted = jnp.where(live_mask[None, :], flux, jnp.float32(0.0))
    returned_rows = []
    for row in range(SOURCE_BLOCKS):
        portion = weighted[:, row * SLOT_CAPACITY : (row + 1) * SLOT_CAPACITY]
        if row == RADIUS:
            returned_rows.append(portion)
        else:
            returned_rows.append(passed_along(portion, "atm", RADIUS - row))
    back = jnp.concatenate(returned_rows, axis=1)
    contrib = jnp.where(atm_live[None, :], back, jnp.float32(0.0))
    atm_flux = exact_dot(contrib, atm_picker.astype(jnp.float32))
    entry_flux = exact_dot(theta[None, :] * weighted, pick_one.astype(jnp.float32).T)
    entry_flux = entry_flux + exact_dot(
        (1.0 - theta)[None, :] * weighted, pick_two.astype(jnp.float32).T
    )
    returned = lax.all_to_all(entry_flux, "ocn", split_axis=1, concat_axis=1, tiled=True)
    ocn_flux = exact_dot(returned, ocean_picker.astype(jnp.float32))
    return (atm_flux, ocn_flux)


def solution(mesh):
    placed = (
        P(None, ("atm", "ocn")),
        P(None, ("atm", "ocn")),
        P(),
        P(("atm", "ocn"), None, None),
        P(("atm", "ocn"), None, None),
        P(("atm", "ocn"), None, None),
        P(("atm", "ocn"), None),
        P(("atm", "ocn"), None),
    )
    return jax.shard_map(
        on_device,
        mesh=mesh,
        in_specs=placed,
        out_specs=(P(None, ("atm", "ocn")), P(None, ("atm", "ocn"))),
        check_vma=False,
    )
```

profile of v0, /device:TPU:8, one launch (start us, length us, event | category | flops | bytes accessed | tf_op | source)
XLA Modules:
  0.0 85.9 jit_solution(12492960825442374576)
XLA Ops:
  0.6 0.8 eq.59
  2.7 12.7 %all-to-all-start = ((bf16[64,8,96]{2,0,1:T(8,128)(2,1)}), bf16[64,8,96]{2,0,1:T(8,128)(2,1)S(1)}, u32[]{:S(2)}, u32[]{:S(2)}) async-start(bf16[64,8,96]{2,0,1:T(8,128)(2,1)} %copy.12), calls=%async_computation | async-start | bytes 262144 | tf_op jit(solution)/shard_map/all_to_all | solution.py:61
  15.9 10.7 %collective-permute-start = (bf16[64,64]{1,0:T(8,128)(2,1)S(1)}, bf16[64,64]{1,0:T(8,128)(2,1)S(1)}, u32[]{:S(2)}, u32[]{:S(2)}) collective-permute-start(bf16[64,64]{1,0:T(8,128)(2,1)S(1)} %get-tuple-element.15), channel_id=1, source_target_pairs={{24,0},{32,8},{40,16},{48,24},{56,32},{64,40},{72,48},{80,56},{88,... | collective-permute-start | bytes 24584 | tf_op jit(solution)/shard_map/ppermute | solution.py:15
  26.7 3.0 %collective-permute-start.1 = (bf16[64,64]{1,0:T(8,128)(2,1)S(1)}, bf16[64,64]{1,0:T(8,128)(2,1)S(1)}, u32[]{:S(2)}, u32[]{:S(2)}) collective-permute-start(bf16[64,64]{1,0:T(8,128)(2,1)S(1)} %get-tuple-element.14), channel_id=1, source_target_pairs={{16,0},{24,8},{32,16},{40,24},{48,32},{56,40},{64,48},{72,56},{80,... | collective-permute-start | bytes 24584 | tf_op jit(solution)/shard_map/ppermute | solution.py:15
  29.7 2.4 %collective-permute-start.2 = (bf16[64,64]{1,0:T(8,128)(2,1)S(1)}, bf16[64,64]{1,0:T(8,128)(2,1)S(1)}, u32[]{:S(2)}, u32[]{:S(2)}) collective-permute-start(bf16[64,64]{1,0:T(8,128)(2,1)S(1)} %get-tuple-element.13), channel_id=1, source_target_pairs={{8,0},{16,8},{24,16},{32,24},{40,32},{48,40},{56,48},{64,56},{72,6... | collective-permute-start | bytes 24584 | tf_op jit(solution)/shard_map/ppermute | solution.py:15
  32.2 1.9 %collective-permute-start.3 = (bf16[64,64]{1,0:T(8,128)(2,1)S(1)}, bf16[64,64]{1,0:T(8,128)(2,1)S(1)}, u32[]{:S(2)}, u32[]{:S(2)}) collective-permute-start(bf16[64,64]{1,0:T(8,128)(2,1)S(1)} %get-tuple-element.11), channel_id=1, source_target_pairs={{760,0},{0,8},{8,16},{16,24},{24,32},{32,40},{40,48},{48,56},{56,6... | collective-permute-start | bytes 24584 | tf_op jit(solution)/shard_map/ppermute | solution.py:15
  34.1 3.4 %collective-permute-start.4 = (bf16[64,64]{1,0:T(8,128)(2,1)S(1)}, bf16[64,64]{1,0:T(8,128)(2,1)S(1)}, u32[]{:S(2)}, u32[]{:S(2)}) collective-permute-start(bf16[64,64]{1,0:T(8,128)(2,1)S(1)} %get-tuple-element.10), channel_id=1, source_target_pairs={{752,0},{760,8},{0,16},{8,24},{16,32},{24,40},{32,48},{40,56},{48,... | collective-permute-start | bytes 24584 | tf_op jit(solution)/shard_map/ppermute | solution.py:15
  37.6 2.8 %collective-permute-start.5 = (bf16[64,64]{1,0:T(8,128)(2,1)S(1)}, bf16[64,64]{1,0:T(8,128)(2,1)S(1)}, u32[]{:S(2)}, u32[]{:S(2)}) collective-permute-start(bf16[64,64]{1,0:T(8,128)(2,1)S(1)} %get-tuple-element.9), channel_id=1, source_target_pairs={{744,0},{752,8},{760,16},{0,24},{8,32},{16,40},{24,48},{32,56},{40... | collective-permute-start | bytes 24584 | tf_op jit(solution)/shard_map/ppermute | solution.py:15
  40.6 2.5 %collective-permute-done.4 = bf16[64,64]{1,0:T(8,128)(2,1)S(1)} collective-permute-done((bf16[64,64]{1,0:T(8,128)(2,1)S(1)}, bf16[64,64]{1,0:T(8,128)(2,1)S(1)}, u32[]{:S(2)}, u32[]{:S(2)}) %collective-permute-start.4) | collective-permute-done | bytes 8224 | tf_op jit(solution)/shard_map/ppermute | solution.py:15
  43.1 3.2 %collective-permute-done.5 = bf16[64,64]{1,0:T(8,128)(2,1)S(1)} collective-permute-done((bf16[64,64]{1,0:T(8,128)(2,1)S(1)}, bf16[64,64]{1,0:T(8,128)(2,1)S(1)}, u32[]{:S(2)}, u32[]{:S(2)}) %collective-permute-start.5) | collective-permute-done | bytes 8224 | tf_op jit(solution)/shard_map/ppermute | solution.py:15
  47.9 0.9 %fusion = f32[64,768]{1,0:T(8,128)S(1)} fusion(s32[448]{0:T(512)S(1)} %bitcast.25, f32[64,448]{1,0:T(8,128)S(1)} %multiply_select_fusion, f32[448]{0:T(512)S(1)} %bitcast.23), kind=kOutput, calls=%fused_computation.1 | convolution fusion | flops 264613888 | bytes 314880 | tf_op jit(solution)/shard_map/dot_general | solution.py:38
  48.8 1.9 %collective-permute-start.6 = (f32[64,64]{1,0:T(8,128)S(1)}, f32[64,64]{1,0:T(8,128)S(1)}, u32[]{:S(2)}, u32[]{:S(2)}) collective-permute-start(f32[64,64]{1,0:T(8,128)S(1)} %get-tuple-element.8), channel_id=1, source_target_pairs={{744,0},{752,8},{760,16},{0,24},{8,32},{16,40},{24,48},{32,56},{40... | collective-permute-start | bytes 49160 | tf_op jit(solution)/shard_map/ppermute | solution.py:15
  50.7 3.1 %collective-permute-start.7 = (f32[64,64]{1,0:T(8,128)S(1)}, f32[64,64]{1,0:T(8,128)S(1)}, u32[]{:S(2)}, u32[]{:S(2)}) collective-permute-start(f32[64,64]{1,0:T(8,128)S(1)} %get-tuple-element.7), channel_id=1, source_target_pairs={{752,0},{760,8},{0,16},{8,24},{16,32},{24,40},{32,48},{40,56},{48,... | collective-permute-start | bytes 49160 | tf_op jit(solution)/shard_map/ppermute | solution.py:15
  53.8 1.9 %collective-permute-start.8 = (f32[64,64]{1,0:T(8,128)S(1)}, f32[64,64]{1,0:T(8,128)S(1)}, u32[]{:S(2)}, u32[]{:S(2)}) collective-permute-start(f32[64,64]{1,0:T(8,128)S(1)} %get-tuple-element.6), channel_id=1, source_target_pairs={{760,0},{0,8},{8,16},{16,24},{24,32},{32,40},{40,48},{48,56},{56,6... | collective-permute-start | bytes 49160 | tf_op jit(solution)/shard_map/ppermute | solution.py:15
  55.8 7.0 %collective-permute-start.9 = (f32[64,64]{1,0:T(8,128)S(1)}, f32[64,64]{1,0:T(8,128)S(1)}, u32[]{:S(2)}, u32[]{:S(2)}) collective-permute-start(f32[64,64]{1,0:T(8,128)S(1)} %get-tuple-element.4), channel_id=1, source_target_pairs={{8,0},{16,8},{24,16},{32,24},{40,32},{48,40},{56,48},{64,56},{72,6... | collective-permute-start | bytes 49160 | tf_op jit(solution)/shard_map/ppermute | solution.py:15
  62.7 3.1 %collective-permute-start.10 = (f32[64,64]{1,0:T(8,128)S(1)}, f32[64,64]{1,0:T(8,128)S(1)}, u32[]{:S(2)}, u32[]{:S(2)}) collective-permute-start(f32[64,64]{1,0:T(8,128)S(1)} %get-tuple-element.3), channel_id=1, source_target_pairs={{16,0},{24,8},{32,16},{40,24},{48,32},{56,40},{64,48},{72,56},{80,... | collective-permute-start | bytes 49160 | tf_op jit(solution)/shard_map/ppermute | solution.py:15
  65.8 0.9 %fusion.6 = f32[64,768]{1,0:T(8,128)S(1)} fusion(f32[64,768]{1,0:T(8,128)S(1)} %fusion, s32[448]{0:T(512)S(1)} %bitcast.17, f32[64,448]{1,0:T(8,128)S(1)} %multiply_select_fusion, f32[448]{0:T(512)S(1)} %bitcast.21), kind=kOutput, calls=%fused_computation.9 | convolution fusion | flops 264663040 | bytes 511488 | tf_op jit(solution)/shard_map/dot_general | solution.py:38
  66.9 0.7 copy.14
  67.7 7.2 %all-to-all-start.1 = ((f32[64,8,96]{2,0,1:T(8,128)}), f32[64,8,96]{2,0,1:T(8,128)S(1)}, u32[]{:S(2)}, u32[]{:S(2)}) async-start(f32[64,8,96]{2,0,1:T(8,128)} %copy.14), calls=%async_computation.1 | async-start | bytes 524288 | tf_op jit(solution)/shard_map/all_to_all | solution.py:91
  74.9 2.5 %collective-permute-start.11 = (f32[64,64]{1,0:T(8,128)S(1)}, f32[64,64]{1,0:T(8,128)S(1)}, u32[]{:S(2)}, u32[]{:S(2)}) collective-permute-start(f32[64,64]{1,0:T(8,128)S(1)} %get-tuple-element.2), channel_id=1, source_target_pairs={{24,0},{32,8},{40,16},{48,24},{56,32},{64,40},{72,48},{80,56},{88,... | collective-permute-start | bytes 49160 | tf_op jit(solution)/shard_map/ppermute | solution.py:15
  77.4 2.7 %collective-permute-done.11 = f32[64,64]{1,0:T(8,128)S(1)} collective-permute-done((f32[64,64]{1,0:T(8,128)S(1)}, f32[64,64]{1,0:T(8,128)S(1)}, u32[]{:S(2)}, u32[]{:S(2)}) %collective-permute-start.11) | collective-permute-done | bytes 16416 | tf_op jit(solution)/shard_map/ppermute | solution.py:15
  80.2 1.0 %fusion.21 = f32[64,256]{1,0:T(8,128)} fusion(s32[448]{0:T(512)S(1)} %reshape.26, f32[64,448]{1,0:T(8,128)S(1)} %concatenate.7, pred[448]{0:T(512)(128)(4,1)S(1)} %broadcast_compare_fusion.1), kind=kOutput, calls=%fused_computation.26 | convolution fusion | flops 88223744 | bytes 182464 | tf_op jit(solution)/shard_map/dot_general | solution.py:38
  81.2 3.2 %all-to-all-done.1 = f32[64,8,96]{2,0,1:T(8,128)S(1)} async-done(((f32[64,8,96]{2,0,1:T(8,128)}), f32[64,8,96]{2,0,1:T(8,128)S(1)}, u32[]{:S(2)}, u32[]{:S(2)}) %all-to-all-start.1) | async-done | bytes 196640 | tf_op jit(solution)/shard_map/all_to_all | solution.py:91
  84.7 1.3 %fusion.4 = f32[64,384]{1,0:T(8,128)} fusion(f32[64,768]{1,0:T(8,128)S(1)} %all_to_all.21, s32[768]{0:T(1024)S(1)} %eq.59), kind=kOutput, calls=%fused_computation.7 | convolution fusion | flops 226787328 | bytes 297984 | tf_op jit(solution)/shard_map/dot_general | solution.py:38
  (50 shorter events, 4.0 us)
Async XLA Ops:
  0.6 0.8 copy-start
  2.0 13.4 %copy-start.3 = (s32[1,7,64]{2,0,1:T(1,128)S(1)}, s32[1,7,64]{2,0,1:T(1,128)}, u32[]{:S(2)}) copy-start(s32[1,7,64]{2,0,1:T(1,128)} %param.11) | copy-start | bytes 5380
  2.0 13.5 %copy-start.6 = (bf16[64,256]{1,0:T(8,128)(2,1)S(1)}, bf16[64,256]{1,0:T(8,128)(2,1)}, u32[]{:S(2)}) copy-start(bf16[64,256]{1,0:T(8,128)(2,1)} %param.8) | copy-start | bytes 98308
  2.7 43.7 %all-to-all-start = ((bf16[64,8,96]{2,0,1:T(8,128)(2,1)}), bf16[64,8,96]{2,0,1:T(8,128)(2,1)S(1)}, u32[]{:S(2)}, u32[]{:S(2)}) async-start(bf16[64,8,96]{2,0,1:T(8,128)(2,1)} %copy.12), calls=%async_computation | async-start | bytes 262144 | tf_op jit(solution)/shard_map/all_to_all | solution.py:61
  15.4 22.1 %copy-start.2 = (s32[1,2,448]{2,1,0:T(2,128)S(1)}, s32[1,2,448]{2,1,0:T(2,128)}, u32[]{:S(2)}) copy-start(s32[1,2,448]{2,1,0:T(2,128)} %param.13) | copy-start | bytes 10756
  15.4 22.1 %copy-start.1 = (bf16[1,448]{1,0:T(2,128)(2,1)S(1)}, bf16[1,448]{1,0:T(2,128)(2,1)}, u32[]{:S(2)}) copy-start(bf16[1,448]{1,0:T(2,128)(2,1)} %param.15) | copy-start | bytes 2692
  15.5 25.0 %copy-start.4 = (bf16[1,448]{1,0:T(2,128)(2,1)S(1)}, bf16[1,448]{1,0:T(2,128)(2,1)}, u32[]{:S(2)}) copy-start(bf16[1,448]{1,0:T(2,128)(2,1)} %param.14) | copy-start | bytes 2692
  15.9 21.6 %collective-permute-start = (bf16[64,64]{1,0:T(8,128)(2,1)S(1)}, bf16[64,64]{1,0:T(8,128)(2,1)S(1)}, u32[]{:S(2)}, u32[]{:S(2)}) collective-permute-start(bf16[64,64]{1,0:T(8,128)(2,1)S(1)} %get-tuple-element.15), channel_id=1, source_target_pairs={{24,0},{32,8},{40,16},{48,24},{56,32},{64,40},{72,48},{80,56},{88,... | collective-permute-start | bytes 24584 | tf_op jit(solution)/shard_map/ppermute | solution.py:15
  26.7 13.8 %collective-permute-start.1 = (bf16[64,64]{1,0:T(8,128)(2,1)S(1)}, bf16[64,64]{1,0:T(8,128)(2,1)S(1)}, u32[]{:S(2)}, u32[]{:S(2)}) collective-permute-start(bf16[64,64]{1,0:T(8,128)(2,1)S(1)} %get-tuple-element.14), channel_id=1, source_target_pairs={{16,0},{24,8},{32,16},{40,24},{48,32},{56,40},{64,48},{72,56},{80,... | collective-permute-start | bytes 24584 | tf_op jit(solution)/shard_map/ppermute | solution.py:15
  29.7 10.7 %collective-permute-start.2 = (bf16[64,64]{1,0:T(8,128)(2,1)S(1)}, bf16[64,64]{1,0:T(8,128)(2,1)S(1)}, u32[]{:S(2)}, u32[]{:S(2)}) collective-permute-start(bf16[64,64]{1,0:T(8,128)(2,1)S(1)} %get-tuple-element.13), channel_id=1, source_target_pairs={{8,0},{16,8},{24,16},{32,24},{40,32},{48,40},{56,48},{64,56},{72,6... | collective-permute-start | bytes 24584 | tf_op jit(solution)/shard_map/ppermute | solution.py:15
  32.2 8.4 %collective-permute-start.3 = (bf16[64,64]{1,0:T(8,128)(2,1)S(1)}, bf16[64,64]{1,0:T(8,128)(2,1)S(1)}, u32[]{:S(2)}, u32[]{:S(2)}) collective-permute-start(bf16[64,64]{1,0:T(8,128)(2,1)S(1)} %get-tuple-element.11), channel_id=1, source_target_pairs={{760,0},{0,8},{8,16},{16,24},{24,32},{32,40},{40,48},{48,56},{56,6... | collective-permute-start | bytes 24584 | tf_op jit(solution)/shard_map/ppermute | solution.py:15
  34.1 9.0 %collective-permute-start.4 = (bf16[64,64]{1,0:T(8,128)(2,1)S(1)}, bf16[64,64]{1,0:T(8,128)(2,1)S(1)}, u32[]{:S(2)}, u32[]{:S(2)}) collective-permute-start(bf16[64,64]{1,0:T(8,128)(2,1)S(1)} %get-tuple-element.10), channel_id=1, source_target_pairs={{752,0},{760,8},{0,16},{8,24},{16,32},{24,40},{32,48},{40,56},{48,... | collective-permute-start | bytes 24584 | tf_op jit(solution)/shard_map/ppermute | solution.py:15
  37.6 8.7 %collective-permute-start.5 = (bf16[64,64]{1,0:T(8,128)(2,1)S(1)}, bf16[64,64]{1,0:T(8,128)(2,1)S(1)}, u32[]{:S(2)}, u32[]{:S(2)}) collective-permute-start(bf16[64,64]{1,0:T(8,128)(2,1)S(1)} %get-tuple-element.9), channel_id=1, source_target_pairs={{744,0},{752,8},{760,16},{0,24},{8,32},{16,40},{24,48},{32,56},{40... | collective-permute-start | bytes 24584 | tf_op jit(solution)/shard_map/ppermute | solution.py:15
  47.0 0.7 copy-start.5
  48.8 26.1 %collective-permute-start.6 = (f32[64,64]{1,0:T(8,128)S(1)}, f32[64,64]{1,0:T(8,128)S(1)}, u32[]{:S(2)}, u32[]{:S(2)}) collective-permute-start(f32[64,64]{1,0:T(8,128)S(1)} %get-tuple-element.8), channel_id=1, source_target_pairs={{744,0},{752,8},{760,16},{0,24},{8,32},{16,40},{24,48},{32,56},{40... | collective-permute-start | bytes 49160 | tf_op jit(solution)/shard_map/ppermute | solution.py:15
  50.7 26.7 %collective-permute-start.7 = (f32[64,64]{1,0:T(8,128)S(1)}, f32[64,64]{1,0:T(8,128)S(1)}, u32[]{:S(2)}, u32[]{:S(2)}) collective-permute-start(f32[64,64]{1,0:T(8,128)S(1)} %get-tuple-element.7), channel_id=1, source_target_pairs={{752,0},{760,8},{0,16},{8,24},{16,32},{24,40},{32,48},{40,56},{48,... | collective-permute-start | bytes 49160 | tf_op jit(solution)/shard_map/ppermute | solution.py:15
  53.8 23.6 %collective-permute-start.8 = (f32[64,64]{1,0:T(8,128)S(1)}, f32[64,64]{1,0:T(8,128)S(1)}, u32[]{:S(2)}, u32[]{:S(2)}) collective-permute-start(f32[64,64]{1,0:T(8,128)S(1)} %get-tuple-element.6), channel_id=1, source_target_pairs={{760,0},{0,8},{8,16},{16,24},{24,32},{32,40},{40,48},{48,56},{56,6... | collective-permute-start | bytes 49160 | tf_op jit(solution)/shard_map/ppermute | solution.py:15
  55.8 21.6 %collective-permute-start.9 = (f32[64,64]{1,0:T(8,128)S(1)}, f32[64,64]{1,0:T(8,128)S(1)}, u32[]{:S(2)}, u32[]{:S(2)}) collective-permute-start(f32[64,64]{1,0:T(8,128)S(1)} %get-tuple-element.4), channel_id=1, source_target_pairs={{8,0},{16,8},{24,16},{32,24},{40,32},{48,40},{56,48},{64,56},{72,6... | collective-permute-start | bytes 49160 | tf_op jit(solution)/shard_map/ppermute | solution.py:15
  62.7 14.7 %collective-permute-start.10 = (f32[64,64]{1,0:T(8,128)S(1)}, f32[64,64]{1,0:T(8,128)S(1)}, u32[]{:S(2)}, u32[]{:S(2)}) collective-permute-start(f32[64,64]{1,0:T(8,128)S(1)} %get-tuple-element.3), channel_id=1, source_target_pairs={{16,0},{24,8},{32,16},{40,24},{48,32},{56,40},{64,48},{72,56},{80,... | collective-permute-start | bytes 49160 | tf_op jit(solution)/shard_map/ppermute | solution.py:15
  67.7 16.7 %all-to-all-start.1 = ((f32[64,8,96]{2,0,1:T(8,128)}), f32[64,8,96]{2,0,1:T(8,128)S(1)}, u32[]{:S(2)}, u32[]{:S(2)}) async-start(f32[64,8,96]{2,0,1:T(8,128)} %copy.14), calls=%async_computation.1 | async-start | bytes 524288 | tf_op jit(solution)/shard_map/all_to_all | solution.py:91
  74.9 5.2 %collective-permute-start.11 = (f32[64,64]{1,0:T(8,128)S(1)}, f32[64,64]{1,0:T(8,128)S(1)}, u32[]{:S(2)}, u32[]{:S(2)}) collective-permute-start(f32[64,64]{1,0:T(8,128)S(1)} %get-tuple-element.2), channel_id=1, source_target_pairs={{24,0},{32,8},{40,16},{48,24},{56,32},{64,40},{72,48},{80,56},{88,... | collective-permute-start | bytes 49160 | tf_op jit(solution)/shard_map/ppermute | solution.py:15
where the time goes:
time: 86.6 us; the launch traced here: 85.9 us
  starting transfers between devices  63.8 us (74%)
  waiting for transfers between devices  11.7 us (14%)
  matrix products  5.58 us (6%)
  local copies, waits for them, and re-layouts  3.68 us (4%)
  between operations  0.99 us (1%)
    ppermute x12, starting transfers between devices, passed_along(): return lax.ppermute(block, axis, route)  43.8 us
    all_to_all x1, starting transfers between devices, on_device(): lax.all_to_all(sending, 'ocn', split_axis=1, concat_axis=1, tiled=True)  12.7 us
    ppermute x12, waiting for transfers between devices, passed_along(): return lax.ppermute(block, axis, route)  8.47 us
    all_to_all x1, starting transfers between devices, on_device(): lax.all_to_all(entry_flux, 'ocn', split_axis=1, concat_axis=1, tiled=True)  7.2 us
    dot_general x4, matrix products, exact_dot(): jnp.dot(left, right, precision=lax.Precision.HIGHEST, preferred_element_t...  4.09 us
    all_to_all x1, waiting for transfers between devices, on_device(): lax.all_to_all(entry_flux, 'ocn', split_axis=1, concat_axis=1, tiled=True)  3.22 us
  transfers between devices with their start and end apart: 14, of which 5 were waited for; matrix products, arithmetic and copies ran while one was open for 4% of the time, Pallas kernels for 0%

commit v1 on v0

v1 whole, which is shorter than its diff:
```python
import functools
import jax
import jax.numpy as jnp
from jax import lax
from jax.experimental import pallas as pl
from jax.experimental.pallas import tpu as pltpu
from jax.sharding import Mesh, PartitionSpec as P

NF = 64
RADIUS = 3
CAP = 64
ITERS = 3
ROWS = 7
SLOTS = ROWS * CAP
W = 8
Y = 8
OCAP = 96
PAD = 128
EPAD = Y * PAD
ATM = 256
OCN = 384
MSG = NF + 16
BF = jnp.bfloat16
F32 = jnp.float32
VMEM = pl.BlockSpec(memory_space=pltpu.VMEM)
SMEM = pl.BlockSpec(memory_space=pltpu.SMEM)
NT = (((1,), (1,)), ((), ()))


def one_hot(rows, index):
    ids = lax.broadcasted_iota(jnp.int32, (rows, index.shape[1]), 0)
    return jnp.where(ids == index, 1.0, 0.0).astype(BF)


def entry_row(slots_ref, padded):
    padded[...] = jnp.full((Y, PAD), -1, jnp.int32)
    padded[:, :OCAP] = slots_ref[...]
    return jnp.concatenate([padded[o : o + 1, :] for o in range(Y)], axis=1)


def slot_row(slots_ref):
    return jnp.concatenate([slots_ref[k : k + 1, :] for k in range(ROWS)], axis=1)


def padded_entries(index):
    moved = index
    for o in range(1, Y):
        moved = moved + jnp.where(index >= o * OCAP, PAD - OCAP, 0)
    return moved


def flux(air, sea, scale, area, live):
    du = air[1:2] - sea[1:2]
    dv = air[2:3] - sea[2:3]
    square = du * du + dv * dv + 0.25
    speed = jnp.sqrt(square)
    contrast = air[0:1] - sea[0:1]
    coeff = jnp.ones_like(speed)
    for step in range(ITERS):
        coeff = 1.5 - 0.8 * jnp.tanh(0.3 * contrast * coeff / (speed * speed))
    factor = jnp.where(live, area * (coeff * speed), 0.0)
    return factor * (scale * (air - sea))


def halves(values):
    high = values.astype(BF)
    low = (values - high.astype(F32)).astype(BF)
    return jnp.concatenate([high, low], axis=0)


def summed_onto(values, picker):
    both = lax.dot_general(halves(values), picker, NT, preferred_element_type=F32)
    return both[:NF] + both[NF:]


def send_sea_kernel(fields_ref, slots_ref, out_ref, padded):
    picked = jnp.dot(
        fields_ref[...], one_hot(OCN, entry_row(slots_ref, padded)), preferred_element_type=F32
    ).astype(BF)
    for o in range(Y):
        out_ref[o] = picked[:, o * PAD : o * PAD + OCAP]


def send_air_kernel(place_ref, fields_ref, slots_ref, air_ref, own_ref, cross_ref):
    w = place_ref[0]
    picked = jnp.dot(
        fields_ref[...], one_hot(ATM, slot_row(slots_ref)), preferred_element_type=F32
    )
    air_ref[...] = picked.astype(BF)
    for k in range(ROWS):
        own_ref[lax.rem(w + (k - RADIUS + W), W)] = picked[:, k * CAP : (k + 1) * CAP].astype(BF)
    own_ref[lax.rem(w + W // 2, W)] = jnp.zeros((NF, CAP), BF)
    for j in range(RADIUS):
        cross_ref[j] = jnp.where(w >= W // 2, own_ref[j], own_ref[W - RADIUS + j])


def make_message_kernel(
    place_ref, entries_ref, ocean_ref, theta_ref, area_ref, own_ref, crossed_ref, sea_ref, msg_ref, table
):
    w = place_ref[0]
    table[...] = jnp.zeros((NF, EPAD), BF)
    for o in range(Y):
        table[:, o * PAD : o * PAD + OCAP] = entries_ref[o]
    index = padded_entries(ocean_ref[...])
    entries = table[...]
    first = jnp.dot(entries, one_hot(EPAD, index[0:1]), preferred_element_type=F32)
    second = jnp.dot(entries, one_hot(EPAD, index[1:2]), preferred_element_type=F32)
    theta = theta_ref[...].astype(F32)
    sea = theta * first + (1.0 - theta) * second
    sea_ref[...] = sea.astype(BF)
    area = jnp.broadcast_to(area_ref[...].astype(F32), (MSG - NF, SLOTS))
    both = jnp.concatenate([sea, area], axis=0)
    for p in range(W):
        mine = own_ref[p]
        if p < RADIUS:
            mine = jnp.where(w - p > W // 2, crossed_ref[p], mine)
        if p >= W - RADIUS:
            mine = jnp.where(p - w > W // 2, crossed_ref[p - (W - RADIUS)], mine)
        msg_ref[p, :NF, :CAP] = mine
        msg_ref[p, NF:, :CAP] = jnp.zeros((MSG - NF, CAP), BF)
    for k in range(ROWS):
        msg_ref[lax.rem(w + (RADIUS - k + W), W), :, CAP:] = both[:, k * CAP : (k + 1) * CAP].astype(BF)
    msg_ref[lax.rem(w + W // 2, W), :, CAP:] = jnp.zeros((MSG, CAP), BF)


def entry_flux_kernel(
    place_ref, got_ref, sea_ref, ocean_ref, theta_ref, area_ref, scale_ref, out_ref
):
    w = place_ref[0]
    air = jnp.concatenate(
        [got_ref[lax.rem(w + (RADIUS - k + W), W), :NF, :CAP].astype(F32) for k in range(ROWS)], axis=1
    )
    ocean = ocean_ref[...]
    weighted = flux(
        air, sea_ref[...].astype(F32), scale_ref[...], area_ref[...].astype(F32), ocean[0:1] >= 0
    )
    index = padded_entries(ocean)
    theta = theta_ref[...].astype(F32)
    total = summed_onto(theta * weighted, one_hot(EPAD, index[0:1]))
    total = total + summed_onto((1.0 - theta) * weighted, one_hot(EPAD, index[1:2]))
    total = total.astype(BF)
    for o in range(Y):
        out_ref[o] = total[:, o * PAD : o * PAD + OCAP]


def atm_flux_kernel(place_ref, got_ref, crossed_ref, air_ref, slots_ref, scale_ref, out_ref):
    w = place_ref[0]
    parts = []
    for k in range(ROWS):
        p = lax.rem(w + (k - RADIUS + W), W)
        here = got_ref[p, :, CAP:]
        there = jnp.where(p >= W - RADIUS, p - (W - RADIUS), jnp.minimum(p, RADIUS - 1))
        away = crossed_ref[there, :, CAP:]
        over = w + (k - RADIUS)
        parts.append(jnp.where((over < 0) | (over >= W), away, here).astype(F32))
    both = jnp.concatenate(parts, axis=1)
    index = slot_row(slots_ref)
    weighted = flux(
        air_ref[...].astype(F32), both[:NF], scale_ref[...], both[NF : NF + 1], index >= 0
    )
    out_ref[...] = summed_onto(weighted, one_hot(ATM, index))


def ocn_flux_kernel(got_ref, slots_ref, out_ref, padded, table):
    table[...] = jnp.zeros((NF, EPAD), BF)
    for o in range(Y):
        table[:, o * PAD : o * PAD + OCAP] = got_ref[o]
    picker = one_hot(OCN, entry_row(slots_ref, padded))
    out_ref[...] = lax.dot_general(table[...], picker, NT, preferred_element_type=F32)


def call(kernel, name, ins, outs, scratch=(), scalar=True):
    specs = [SMEM] + [VMEM] * (len(ins) - 1) if scalar else [VMEM] * len(ins)
    single = len(outs) == 1
    shapes = [jax.ShapeDtypeStruct(s, d) for s, d in outs]
    return pl.pallas_call(
        kernel,
        out_shape=shapes[0] if single else shapes,
        in_specs=specs,
        out_specs=VMEM if single else [VMEM] * len(outs),
        scratch_shapes=list(scratch),
        name=name,
        compiler_params=pltpu.CompilerParams(vmem_limit_bytes=24 * 1024 * 1024),
    )(*ins)


def on_device(
    planes, atm_fields, ocn_fields, transfer_scale, atmosphere_slots, ocn_slots, xc_ocean, xc_area, xc_theta
):
    w = lax.axis_index("w")
    place = w.reshape(1).astype(jnp.int32)
    atm_slots = atmosphere_slots[0]
    sea_slots = ocn_slots[0]
    ocean = xc_ocean[0]
    scale = transfer_scale[:, None]
    index_pad = pltpu.VMEM((Y, PAD), jnp.int32)
    table = pltpu.VMEM((NF, EPAD), BF)

    sending = call(
        send_sea_kernel, "send_sea", (ocn_fields, sea_slots), [((Y, NF, OCAP), BF)], [index_pad], scalar=False
    )
    entries = lax.all_to_all(sending, "ocn", 0, 0, tiled=True)

    air, own, cross = call(
        send_air_kernel,
        "send_air",
        (place, atm_fields, atm_slots),
        [((NF, SLOTS), BF), ((W, NF, CAP), BF), ((RADIUS, NF, CAP), BF)],
    )
    up, down = [], []
    for z in range(planes):
        for v in range(W):
            here, above, below = z * W + v, (z + 1) % planes * W + v, (z - 1) % planes * W + v
            if v >= W - RADIUS:
                up.append((here, above))
                down.append((here, below))
            if v < RADIUS:
                up.append((here, below))
                down.append((here, above))
    crossed = lax.ppermute(cross, ("z", "w"), up)

    sea, message = call(
        make_message_kernel,
        "make_message",
        (place, entries, ocean, xc_theta, xc_area, own, crossed),
        [((NF, SLOTS), BF), ((W, MSG, 2 * CAP), BF)],
        [table],
    )
    got = lax.all_to_all(message, "w", 0, 0, tiled=True)

    entry = call(
        entry_flux_kernel,
        "entry_flux",
        (place, got, sea, ocean, xc_theta, xc_area, scale),
        [((Y, NF, OCAP), BF)],
    )
    returned = lax.all_to_all(entry, "ocn", 0, 0, tiled=True)
    back = lax.ppermute(jnp.where(w < W // 2, got[W - RADIUS :], got[:RADIUS]), ("z", "w"), down)
    atm_flux = call(
        atm_flux_kernel,
        "atm_flux",
        (place, got, back, air, atm_slots, scale),
        [((NF, ATM), F32)],
    )
    ocn_flux = call(
        ocn_flux_kernel, "ocn_flux", (returned, sea_slots), [((NF, OCN), F32)], [index_pad, table], scalar=False
    )
    return (atm_flux, ocn_flux)


def solution(mesh):
    n_atm, n_ocn = mesh.shape["atm"], mesh.shape["ocn"]
    planes = n_atm // W
    split = Mesh(mesh.devices.reshape(planes, W, n_ocn), ("z", "w", "ocn"))
    every = ("z", "w", "ocn")
    placed = (
        P(None, every),
        P(None, every),
        P(),
        P(every, None, None),
        P(every, None, None),
        P(every, None, None),
        P(every, None),
        P(every, None),
    )
    return jax.shard_map(
        functools.partial(on_device, planes),
        mesh=split,
        in_specs=placed,
        out_specs=(P(None, every), P(None, every)),
        check_vma=False,
    )
```

time: 86.6 us -> 59.1 us (0.68)
  starting transfers between devices: 63.8 us -> 35.8 us
  Pallas kernels: 0 us -> 6.16 us
  matrix products: 5.58 us -> 0 us
  waiting for transfers between devices: 11.7 us -> 12.9 us
    ppermute x12 -> x2, starting transfers between devices: 43.8 us -> 11.3 us  [the longest x1 9.4 us: on_device(): crossed = lax.ppermute(cross, ('z', 'w'), up)]
    pallas_call x0 -> x6, Pallas kernels: none -> 6.16 us  [call(): pl.pallas_call(kernel, out_shape=shapes[0] if single else shapes, in_spec...]
    dot_general x8 -> x0, matrix products: 5.58 us -> none  [the longest x4 4.09 us: exact_dot(): jnp.dot(left, right, precision=lax.Precision.HIGHEST, preferred_element_t...]
    all_to_all x2 -> x3, starting transfers between devices: 19.9 us -> 24.4 us  [the longest x1 12.9 us: on_device(): entries = lax.all_to_all(sending, 'ocn', 0, 0, tiled=True)]
    unnamed x14 -> x19, local copies, waits for them, and re-layouts: 0.23 us -> 2.84 us
    all_to_all x2 -> x3, waiting for transfers between devices: 3.22 us -> 5.74 us  [the longest x1 5.73 us: on_device(): got = lax.all_to_all(message, 'w', 0, 0, tiled=True)]
    all_to_all x8 -> x0, local copies, waits for them, and re-layouts: 2.21 us -> none  [the longest x4 1.16 us: on_device(): lax.all_to_all(entry_flux, 'ocn', split_axis=1, concat_axis=1, tiled=True)]
    ppermute x12 -> x2, waiting for transfers between devices: 8.47 us -> 7.13 us  [the longest x1 5.4 us: on_device(): lax.ppermute(jnp.where(w < W // 2, got[W - RADIUS:], got[:RADIUS]), ('z',...]
  transfers between devices with their start and end apart: 14 -> 5, of which waited for: 5 -> 3; matrix products, arithmetic and copies ran while one was open for 4% -> 0% of each run, Pallas kernels for 0% -> 2%
where the time goes in v1:
time: 59.1 us; the launch traced here: 58.4 us
  starting transfers between devices  35.8 us (61%)
  waiting for transfers between devices  12.9 us (22%)
  Pallas kernels  6.16 us (10%)
  local copies, waits for them, and re-layouts  2.93 us (5%)
  between operations  0.7 us (1%)
    all_to_all x1, starting transfers between devices, on_device(): entries = lax.all_to_all(sending, 'ocn', 0, 0, tiled=True)  12.9 us
    ppermute x1, starting transfers between devices, on_device(): crossed = lax.ppermute(cross, ('z', 'w'), up)  9.4 us
    all_to_all x1, starting transfers between devices, on_device(): returned = lax.all_to_all(entry, 'ocn', 0, 0, tiled=True)  7.21 us
    pallas_call x6, Pallas kernels, call(): pl.pallas_call(kernel, out_shape=shapes[0] if single else shapes, in_spec...  6.16 us
    all_to_all x1, waiting for transfers between devices, on_device(): got = lax.all_to_all(message, 'w', 0, 0, tiled=True)  5.73 us
    ppermute x1, waiting for transfers between devices, on_device(): lax.ppermute(jnp.where(w < W // 2, got[W - RADIUS:], got[:RADIUS]), ('z',...  5.4 us
    all_to_all x1, starting transfers between devices, on_device(): got = lax.all_to_all(message, 'w', 0, 0, tiled=True)  4.36 us
    unnamed x19, local copies, waits for them, and re-layouts  2.84 us
  transfers between devices with their start and end apart: 5, of which 3 were waited for; matrix products, arithmetic and copies ran while one was open for 0% of the time, Pallas kernels for 2%

profile of v1, /device:TPU:8, one launch (start us, length us, event | category | flops | bytes accessed | tf_op | source)
XLA Modules:
  0.0 58.4 jit_solution(2847956765007361624)
XLA Ops:
  0.6 0.0 copy-start
  0.6 0.8 %copy-done = bf16[64,384]{1,0:T(8,128)(2,1)S(1)} copy-done((bf16[64,384]{1,0:T(8,128)(2,1)S(1)}, bf16[64,384]{1,0:T(8,128)(2,1)}, u32[]{:S(2)}) %copy-start) | copy-done | bytes 49176
  1.4 0.7 %copy-done.3 = s32[1,8,96]{2,1,0:T(8,128)S(1)} copy-done((s32[1,8,96]{2,1,0:T(8,128)S(1)}, s32[1,8,96]{2,1,0:T(8,128)}, u32[]{:S(2)}) %copy-start.3) | copy-done | bytes 3096
  2.1 1.0 %send_sea.1 = bf16[8,64,96]{2,1,0:T(8,128)(2,1)} custom-call(bf16[64,384]{1,0:T(8,128)(2,1)S(1)} %copy-done, s32[8,96]{1,0:T(8,128)S(1)} %bitcast.11), custom_call_target="tpu_custom_call" | custom-call | tf_op jit(solution)/shard_map/send_sea/pallas_call | solution.py:176
  3.1 12.9 %all-to-all-start = ((bf16[8,64,96]{2,1,0:T(8,128)(2,1)}), bf16[8,64,96]{2,1,0:T(8,128)(2,1)S(1)}, u32[]{:S(2)}, u32[]{:S(2)}) async-start(bf16[8,64,96]{2,1,0:T(8,128)(2,1)} %send_sea.1), calls=%async_computation | async-start | bytes 262144 | tf_op jit(solution)/shard_map/all_to_all | solution.py:202
  16.0 0.7 %copy-done.7 = s32[1,7,64]{2,0,1:T(1,128)S(1)} copy-done((s32[1,7,64]{2,0,1:T(1,128)S(1)}, s32[1,7,64]{2,0,1:T(1,128)}, u32[]{:S(2)}) %copy-start.7) | copy-done | bytes 1816
  16.7 0.3 send_air.1
  17.0 0.0 copy-start.2
  17.0 9.4 %collective-permute-start = (bf16[3,64,64]{2,1,0:T(8,128)(2,1)S(1)}, bf16[3,64,64]{2,1,0:T(8,128)(2,1)S(1)}, u32[]{:S(2)}, u32[]{:S(2)}) collective-permute-start(bf16[3,64,64]{2,1,0:T(8,128)(2,1)S(1)} %get-tuple-element.8), channel_id=1, source_target_pairs={{0,704},{8,712},{16,720},{40,104},{48,112},{56,120},{64,0},{72,8},... | collective-permute-start | bytes 73736 | tf_op jit(solution)/shard_map/ppermute | solution.py:220
  26.5 1.7 %collective-permute-done.crossed_ref = bf16[3,64,64]{2,1,0:T(8,128)(2,1)S(1)} collective-permute-done((bf16[3,64,64]{2,1,0:T(8,128)(2,1)S(1)}, bf16[3,64,64]{2,1,0:T(8,128)(2,1)S(1)}, u32[]{:S(2)}, u32[]{:S(2)}) %collective-permute-start) | collective-permute-done | bytes 24608 | tf_op jit(solution)/shard_map/ppermute | solution.py:220
  28.2 0.0 all-to-all-done.entries_ref
  28.2 0.0 copy-done.2
  28.2 1.3 %make_message.1 = (bf16[64,448]{1,0:T(8,128)(2,1)S(1)}, bf16[8,80,128]{2,1,0:T(8,128)(2,1)}) custom-call(s32[1]{0:T(128)} %bitcast.place_ref, bf16[8,64,96]{2,1,0:T(8,128)(2,1)S(1)} %all-to-all-done.entries_ref, s32[2,448]{1,0:T(2,128)S(1)} %bitcast.9, bf16[1,448]{1,0:T(2,128)(2,1)S(1)} %copy-done.5, bf16[1,448]{1,0:T(2,128)(2,1)S(1)} %copy-done.6, ...), custom_call_target="tpu_custom_call" | custom-call | tf_op jit(solution)/shard_map/make_message/pallas_call | solution.py:176
  29.5 4.4 %all-to-all-start.1 = ((bf16[8,80,128]{2,1,0:T(8,128)(2,1)}), bf16[8,80,128]{2,1,0:T(8,128)(2,1)S(1)}, u32[]{:S(2)}, u32[]{:S(2)}) async-start(bf16[8,80,128]{2,1,0:T(8,128)(2,1)} %get-tuple-element.9), calls=%async_computation.1 | async-start | bytes 327680 | tf_op jit(solution)/shard_map/all_to_all | solution.py:229
  33.8 0.7 %copy-done.8 = f32[64]{0:T(128)S(1)} copy-done((f32[64]{0:T(128)S(1)}, f32[64]{0:T(128)}, u32[]{:S(2)}) %copy-start.8) | copy-done | bytes 280
  34.5 0.1 copy.10.scale_ref
  34.6 5.7 %all-to-all-done.1.got_ref = bf16[8,80,128]{2,1,0:T(8,128)(2,1)S(1)} async-done(((bf16[8,80,128]{2,1,0:T(8,128)(2,1)}), bf16[8,80,128]{2,1,0:T(8,128)(2,1)S(1)}, u32[]{:S(2)}, u32[]{:S(2)}) %all-to-all-start.1) | async-done | bytes 163872 | tf_op jit(solution)/shard_map/all_to_all | solution.py:229
  40.3 1.6 %entry_flux.1 = bf16[8,64,96]{2,1,0:T(8,128)(2,1)} custom-call(s32[1]{0:T(128)} %bitcast.place_ref, bf16[8,80,128]{2,1,0:T(8,128)(2,1)S(1)} %all-to-all-done.1.got_ref, bf16[64,448]{1,0:T(8,128)(2,1)S(1)} %get-tuple-element.11.sea_ref, s32[2,448]{1,0:T(2,128)S(1)} %bitcast.10, bf16[1,448]{1,0:T(2,128)(2,1)S(1)} %copy-done.5, bf16[1,448]{1,0:T(2,128)(2,1)S(1)} %copy-done.6, ...), custom_call_target="tpu_custom_call" | custom-call | tf_op jit(solution)/shard_map/entry_flux/pallas_call | solution.py:176
  41.9 7.2 %all-to-all-start.2 = ((bf16[8,64,96]{2,1,0:T(8,128)(2,1)}), bf16[8,64,96]{2,1,0:T(8,128)(2,1)S(1)}, u32[]{:S(2)}, u32[]{:S(2)}) async-start(bf16[8,64,96]{2,1,0:T(8,128)(2,1)} %entry_flux.1), calls=%async_computation.2 | async-start | bytes 262144 | tf_op jit(solution)/shard_map/all_to_all | solution.py:237
  49.1 1.9 %collective-permute-start.1 = (bf16[3,80,128]{2,1,0:T(8,128)(2,1)S(1)}, bf16[3,80,128]{2,1,0:T(8,128)(2,1)S(1)}, u32[]{:S(2)}, u32[]{:S(2)}) collective-permute-start(bf16[3,80,128]{2,1,0:T(8,128)(2,1)S(1)} %slice_select_fusion), channel_id=1, source_target_pairs={{0,64},{8,72},{16,80},{40,744},{48,752},{56,760},{64,128},{72,136}... | collective-permute-start | bytes 184328 | tf_op jit(solution)/shard_map/ppermute | solution.py:238
  51.1 5.4 %collective-permute-done.1.crossed_ref = bf16[3,80,128]{2,1,0:T(8,128)(2,1)S(1)} collective-permute-done((bf16[3,80,128]{2,1,0:T(8,128)(2,1)S(1)}, bf16[3,80,128]{2,1,0:T(8,128)(2,1)S(1)}, u32[]{:S(2)}, u32[]{:S(2)}) %collective-permute-start.1) | collective-permute-done | bytes 61472 | tf_op jit(solution)/shard_map/ppermute | solution.py:238
  56.5 0.9 %atm_flux.1 = f32[64,256]{1,0:T(8,128)} custom-call(s32[1]{0:T(128)} %bitcast.place_ref, bf16[8,80,128]{2,1,0:T(8,128)(2,1)S(1)} %all-to-all-done.1.got_ref, bf16[3,80,128]{2,1,0:T(8,128)(2,1)S(1)} %collective-permute-done.1.crossed_ref, bf16[64,448]{1,0:T(8,128)(2,1)S(1)} %get-tuple-element.10.air_ref, s32[7,64]{1,0:T(8,128)S(1)} %bitcast.8, ...), custom_call_target="tpu_custom_call" | custom-call | tf_op jit(solution)/shard_map/atm_flux/pallas_call | solution.py:176
  57.4 0.0 all-to-all-done.2.got_ref
  57.4 1.0 %ocn_flux.1 = f32[64,384]{1,0:T(8,128)} custom-call(bf16[8,64,96]{2,1,0:T(8,128)(2,1)S(1)} %all-to-all-done.2.got_ref, s32[8,96]{1,0:T(8,128)S(1)} %bitcast.12), custom_call_target="tpu_custom_call" | custom-call | tf_op jit(solution)/shard_map/ocn_flux/pallas_call | solution.py:176
  (13 shorter events, 0.0 us)
Async XLA Ops:
  0.6 0.8 %copy-start = (bf16[64,384]{1,0:T(8,128)(2,1)S(1)}, bf16[64,384]{1,0:T(8,128)(2,1)}, u32[]{:S(2)}) copy-start(bf16[64,384]{1,0:T(8,128)(2,1)} %fields_ref.2) | copy-start | bytes 147460
  1.4 0.7 %copy-start.3 = (s32[1,8,96]{2,1,0:T(8,128)S(1)}, s32[1,8,96]{2,1,0:T(8,128)}, u32[]{:S(2)}) copy-start(s32[1,8,96]{2,1,0:T(8,128)} %param.12) | copy-start | bytes 9220
  3.1 13.6 %copy-start.1 = (bf16[64,256]{1,0:T(8,128)(2,1)S(1)}, bf16[64,256]{1,0:T(8,128)(2,1)}, u32[]{:S(2)}) copy-start(bf16[64,256]{1,0:T(8,128)(2,1)} %fields_ref.3) | copy-start | bytes 98308
  3.1 25.1 %all-to-all-start = ((bf16[8,64,96]{2,1,0:T(8,128)(2,1)}), bf16[8,64,96]{2,1,0:T(8,128)(2,1)S(1)}, u32[]{:S(2)}, u32[]{:S(2)}) async-start(bf16[8,64,96]{2,1,0:T(8,128)(2,1)} %send_sea.1), calls=%async_computation | async-start | bytes 262144 | tf_op jit(solution)/shard_map/all_to_all | solution.py:202
  16.0 0.7 %copy-start.7 = (s32[1,7,64]{2,0,1:T(1,128)S(1)}, s32[1,7,64]{2,0,1:T(1,128)}, u32[]{:S(2)}) copy-start(s32[1,7,64]{2,0,1:T(1,128)} %param.11) | copy-start | bytes 5380
  16.7 11.5 %copy-start.5 = (bf16[1,448]{1,0:T(2,128)(2,1)S(1)}, bf16[1,448]{1,0:T(2,128)(2,1)}, u32[]{:S(2)}) copy-start(bf16[1,448]{1,0:T(2,128)(2,1)} %theta_ref.3) | copy-start | bytes 2692
  16.7 11.5 %copy-start.6 = (bf16[1,448]{1,0:T(2,128)(2,1)S(1)}, bf16[1,448]{1,0:T(2,128)(2,1)}, u32[]{:S(2)}) copy-start(bf16[1,448]{1,0:T(2,128)(2,1)} %area_ref.3) | copy-start | bytes 2692
  17.0 11.2 %copy-start.2 = (s32[1,2,448]{2,1,0:T(2,128)S(1)}, s32[1,2,448]{2,1,0:T(2,128)}, u32[]{:S(2)}) copy-start(s32[1,2,448]{2,1,0:T(2,128)} %param.13) | copy-start | bytes 10756
  17.0 11.1 %collective-permute-start = (bf16[3,64,64]{2,1,0:T(8,128)(2,1)S(1)}, bf16[3,64,64]{2,1,0:T(8,128)(2,1)S(1)}, u32[]{:S(2)}, u32[]{:S(2)}) collective-permute-start(bf16[3,64,64]{2,1,0:T(8,128)(2,1)S(1)} %get-tuple-element.8), channel_id=1, source_target_pairs={{0,704},{8,712},{16,720},{40,104},{48,112},{56,120},{64,0},{72,8},... | collective-permute-start | bytes 73736 | tf_op jit(solution)/shard_map/ppermute | solution.py:220
  29.5 10.8 %all-to-all-start.1 = ((bf16[8,80,128]{2,1,0:T(8,128)(2,1)}), bf16[8,80,128]{2,1,0:T(8,128)(2,1)S(1)}, u32[]{:S(2)}, u32[]{:S(2)}) async-start(bf16[8,80,128]{2,1,0:T(8,128)(2,1)} %get-tuple-element.9), calls=%async_computation.1 | async-start | bytes 327680 | tf_op jit(solution)/shard_map/all_to_all | solution.py:229
  33.8 0.7 %copy-start.8 = (f32[64]{0:T(128)S(1)}, f32[64]{0:T(128)}, u32[]{:S(2)}) copy-start(f32[64]{0:T(128)} %param.10) | copy-start | bytes 772
  41.9 15.5 %all-to-all-start.2 = ((bf16[8,64,96]{2,1,0:T(8,128)(2,1)}), bf16[8,64,96]{2,1,0:T(8,128)(2,1)S(1)}, u32[]{:S(2)}, u32[]{:S(2)}) async-start(bf16[8,64,96]{2,1,0:T(8,128)(2,1)} %entry_flux.1), calls=%async_computation.2 | async-start | bytes 262144 | tf_op jit(solution)/shard_map/all_to_all | solution.py:237
  49.1 7.3 %collective-permute-start.1 = (bf16[3,80,128]{2,1,0:T(8,128)(2,1)S(1)}, bf16[3,80,128]{2,1,0:T(8,128)(2,1)S(1)}, u32[]{:S(2)}, u32[]{:S(2)}) collective-permute-start(bf16[3,80,128]{2,1,0:T(8,128)(2,1)S(1)} %slice_select_fusion), channel_id=1, source_target_pairs={{0,64},{8,72},{16,80},{40,744},{48,752},{56,760},{64,128},{72,136}... | collective-permute-start | bytes 184328 | tf_op jit(solution)/shard_map/ppermute | solution.py:238
  56.5 1.0 %copy-start.4 = (s32[1,8,96]{2,1,0:T(8,128)S(1)}, s32[1,8,96]{2,1,0:T(8,128)}, u32[]{:S(2)}) copy-start(s32[1,8,96]{2,1,0:T(8,128)} %param.12) | copy-start | bytes 9220

commit v2 on v1

--- a/solution.py
+++ b/solution.py
@@ -32,16 +32,6 @@
     return jnp.where(ids == index, 1.0, 0.0).astype(BF)
 
 
-def entry_row(slots_ref, padded):
-    padded[...] = jnp.full((Y, PAD), -1, jnp.int32)
-    padded[:, :OCAP] = slots_ref[...]
-    return jnp.concatenate([padded[o : o + 1, :] for o in range(Y)], axis=1)
-
-
-def slot_row(slots_ref):
-    return jnp.concatenate([slots_ref[k : k + 1, :] for k in range(ROWS)], axis=1)
-
-
 def padded_entries(index):
     moved = index
     for o in range(1, Y):
@@ -73,25 +63,52 @@
     return both[:NF] + both[NF:]
 
 
-def send_sea_kernel(fields_ref, slots_ref, out_ref, padded):
-    picked = jnp.dot(
-        fields_ref[...], one_hot(OCN, entry_row(slots_ref, padded)), preferred_element_type=F32
-    ).astype(BF)
+def send_kernel(
+    place_ref, ocn_hbm, entries_hbm, atm_hbm, slots_hbm, ocean_hbm, theta_hbm, area_hbm, scale_hbm,
+    out_ref, own_ref, cross_ref, air_ref, entry_row_ref, slot_row_ref, ocean_ref, theta_ref, area_ref, scale_ref,
+    ocn_ref, entries_ref, atm_ref, slots_ref, row_ref, padded, sems,
+):
+    w = place_ref[0]
+    pairs = [
+        (entries_hbm, entries_ref),
+        (ocn_hbm, ocn_ref),
+        (slots_hbm, slots_ref),
+        (atm_hbm, atm_ref),
+        (ocean_hbm, ocean_ref),
+        (theta_hbm, theta_ref),
+        (area_hbm, area_ref),
+        (scale_hbm, row_ref),
+    ]
+    copies = [pltpu.make_async_copy(a, b, sems.at[i]) for i, (a, b) in enumerate(pairs)]
+    for copy in copies:
+        copy.start()
+    padded[...] = jnp.full((Y, PAD), -1, jnp.int32)
+    copies[0].wait()
+    padded[:, :OCAP] = entries_ref[...]
+    index = jnp.concatenate([padded[o : o + 1, :] for o in range(Y)], axis=1)
+    entry_row_ref[...] = index
+    picker = one_hot(OCN, index)
+    copies[1].wait()
+    picked = jnp.dot(ocn_ref[...], picker, preferred_element_type=F32).astype(BF)
     for o in range(Y):
         out_ref[o] = picked[:, o * PAD : o * PAD + OCAP]
-
-
-def send_air_kernel(place_ref, fields_ref, slots_ref, air_ref, own_ref, cross_ref):
-    w = place_ref[0]
-    picked = jnp.dot(
-        fields_ref[...], one_hot(ATM, slot_row(slots_ref)), preferred_element_type=F32
-    )
-    air_ref[...] = picked.astype(BF)
+    copies[2].wait()
+    index = jnp.concatenate([slots_ref[k] for k in range(ROWS)], axis=1)
+    slot_row_ref[...] = index
+    picker = one_hot(ATM, index)
+    copies[3].wait()
+    air = jnp.dot(atm_ref[...], picker, preferred_element_type=F32)
+    air_ref[...] = air.astype(BF)
     for k in range(ROWS):
-        own_ref[lax.rem(w + (k - RADIUS + W), W)] = picked[:, k * CAP : (k + 1) * CAP].astype(BF)
+        own_ref[lax.rem(w + (k - RADIUS + W), W)] = air[:, k * CAP : (k + 1) * CAP].astype(BF)
     own_ref[lax.rem(w + W // 2, W)] = jnp.zeros((NF, CAP), BF)
-    for j in range(RADIUS):
-        cross_ref[j] = jnp.where(w >= W // 2, own_ref[j], own_ref[W - RADIUS + j])
+    crossing = [jnp.where(w >= W // 2, own_ref[j], own_ref[W - RADIUS + j]).astype(F32) for j in range(RADIUS)]
+    cross_ref[...] = jnp.concatenate(crossing, axis=1).astype(BF)
+    for copy in copies[4:]:
+        copy.wait()
+    rows = lax.broadcasted_iota(jnp.int32, (NF, NF), 0)
+    lanes = lax.broadcasted_iota(jnp.int32, (NF, NF), 1)
+    scale_ref[...] = jnp.sum(jnp.where(rows == lanes, row_ref[...], 0.0), axis=1, keepdims=True)
 
 
 def make_message_kernel(
@@ -112,10 +129,9 @@
     both = jnp.concatenate([sea, area], axis=0)
     for p in range(W):
         mine = own_ref[p]
-        if p < RADIUS:
-            mine = jnp.where(w - p > W // 2, crossed_ref[p], mine)
-        if p >= W - RADIUS:
-            mine = jnp.where(p - w > W // 2, crossed_ref[p - (W - RADIUS)], mine)
+        if p < RADIUS or p >= W - RADIUS:
+            j = p if p < RADIUS else p - (W - RADIUS)
+            mine = jnp.where(jnp.abs(p - w) > W // 2, crossed_ref[:, j * CAP : (j + 1) * CAP], mine)
         msg_ref[p, :NF, :CAP] = mine
         msg_ref[p, NF:, :CAP] = jnp.zeros((MSG - NF, CAP), BF)
     for k in range(ROWS):
@@ -124,7 +140,7 @@
 
 
 def entry_flux_kernel(
-    place_ref, got_ref, sea_ref, ocean_ref, theta_ref, area_ref, scale_ref, out_ref
+    place_ref, got_ref, sea_ref, ocean_ref, theta_ref, area_ref, scale_ref, out_ref, cross_ref
 ):
     w = place_ref[0]
     air = jnp.concatenate(
@@ -141,36 +157,37 @@
     total = total.astype(BF)
     for o in range(Y):
         out_ref[o] = total[:, o * PAD : o * PAD + OCAP]
-
-
-def atm_flux_kernel(place_ref, got_ref, crossed_ref, air_ref, slots_ref, scale_ref, out_ref):
+    first = jnp.where(w < W // 2, W - RADIUS, 0)
+    crossing = [got_ref[first + j, :, CAP:].astype(F32) for j in range(RADIUS)]
+    cross_ref[...] = jnp.concatenate(crossing, axis=1).astype(BF)
+
+
+def atm_flux_kernel(place_ref, got_ref, crossed_ref, air_ref, slots_ref, scale_ref, out_ref, spread):
     w = place_ref[0]
-    parts = []
-    for k in range(ROWS):
-        p = lax.rem(w + (k - RADIUS + W), W)
+    for p in range(W):
         here = got_ref[p, :, CAP:]
-        there = jnp.where(p >= W - RADIUS, p - (W - RADIUS), jnp.minimum(p, RADIUS - 1))
-        away = crossed_ref[there, :, CAP:]
-        over = w + (k - RADIUS)
-        parts.append(jnp.where((over < 0) | (over >= W), away, here).astype(F32))
-    both = jnp.concatenate(parts, axis=1)
-    index = slot_row(slots_ref)
+        if p < RADIUS or p >= W - RADIUS:
+            j = p if p < RADIUS else p - (W - RADIUS)
+            here = jnp.where(jnp.abs(p - w) > W // 2, crossed_ref[:, j * CAP : (j + 1) * CAP], here)
+        spread[p] = here.astype(F32)
+    both = jnp.concatenate([spread[lax.rem(w + (k - RADIUS + W), W)] for k in range(ROWS)], axis=1)
+    index = slots_ref[...]
     weighted = flux(
         air_ref[...].astype(F32), both[:NF], scale_ref[...], both[NF : NF + 1], index >= 0
     )
     out_ref[...] = summed_onto(weighted, one_hot(ATM, index))
 
 
-def ocn_flux_kernel(got_ref, slots_ref, out_ref, padded, table):
+def ocn_flux_kernel(place_ref, returned_ref, entries_ref, out_ref, table):
     table[...] = jnp.zeros((NF, EPAD), BF)
     for o in range(Y):
-        table[:, o * PAD : o * PAD + OCAP] = got_ref[o]
-    picker = one_hot(OCN, entry_row(slots_ref, padded))
+        table[:, o * PAD : o * PAD + OCAP] = returned_ref[o]
+    picker = one_hot(OCN, entries_ref[...])
     out_ref[...] = lax.dot_general(table[...], picker, NT, preferred_element_type=F32)
 
 
-def call(kernel, name, ins, outs, scratch=(), scalar=True):
-    specs = [SMEM] + [VMEM] * (len(ins) - 1) if scalar else [VMEM] * len(ins)
+def call(kernel, name, ins, outs, scratch=(), space=pltpu.VMEM):
+    specs = [SMEM] + [pl.BlockSpec(memory_space=space)] * (len(ins) - 1)
     single = len(outs) == 1
     shapes = [jax.ShapeDtypeStruct(s, d) for s, d in outs]
     return pl.pallas_call(
@@ -189,23 +206,43 @@
 ):
     w = lax.axis_index("w")
     place = w.reshape(1).astype(jnp.int32)
-    atm_slots = atmosphere_slots[0]
-    sea_slots = ocn_slots[0]
-    ocean = xc_ocean[0]
-    scale = transfer_scale[:, None]
-    index_pad = pltpu.VMEM((Y, PAD), jnp.int32)
     table = pltpu.VMEM((NF, EPAD), BF)
-
-    sending = call(
-        send_sea_kernel, "send_sea", (ocn_fields, sea_slots), [((Y, NF, OCAP), BF)], [index_pad], scalar=False
-    )
-    entries = lax.all_to_all(sending, "ocn", 0, 0, tiled=True)
-
-    air, own, cross = call(
-        send_air_kernel,
-        "send_air",
-        (place, atm_fields, atm_slots),
-        [((NF, SLOTS), BF), ((W, NF, CAP), BF), ((RADIUS, NF, CAP), BF)],
+    given = (
+        ocn_fields,
+        ocn_slots[0],
+        atm_fields,
+        atmosphere_slots.reshape(ROWS, 1, CAP),
+        xc_ocean[0],
+        xc_theta,
+        xc_area,
+        transfer_scale[None, :],
+    )
+    sending, own, cross, air, entry_row, slot_row, ocean, theta, area, scale = call(
+        send_kernel,
+        "send",
+        (place, *(pltpu.with_memory_space_constraint(x, pltpu.HBM) for x in given)),
+        [
+            ((Y, NF, OCAP), BF),
+            ((W, NF, CAP), BF),
+            ((NF, RADIUS * CAP), BF),
+            ((NF, SLOTS), BF),
+            ((1, EPAD), jnp.int32),
+            ((1, SLOTS), jnp.int32),
+            ((2, SLOTS), jnp.int32),
+            ((1, SLOTS), BF),
+            ((1, SLOTS), BF),
+            ((NF, 1), F32),
+        ],
+        [
+            pltpu.VMEM((NF, OCN), BF),
+            pltpu.VMEM((Y, OCAP), jnp.int32),
+            pltpu.VMEM((NF, ATM), BF),
+            pltpu.VMEM((ROWS, 1, CAP), jnp.int32),
+            pltpu.VMEM((1, NF), F32),
+            pltpu.VMEM((Y, PAD), jnp.int32),
+            pltpu.SemaphoreType.DMA((8,)),
+        ],
+        pltpu.HBM,
     )
     up, down = [], []
     for z in range(planes):
@@ -217,34 +254,32 @@
             if v < RADIUS:
                 up.append((here, below))
                 down.append((here, above))
+    entries = lax.all_to_all(sending, "ocn", 0, 0, tiled=True)
     crossed = lax.ppermute(cross, ("z", "w"), up)
-
     sea, message = call(
         make_message_kernel,
         "make_message",
-        (place, entries, ocean, xc_theta, xc_area, own, crossed),
+        (place, entries, ocean, theta, area, own, crossed),
         [((NF, SLOTS), BF), ((W, MSG, 2 * CAP), BF)],
         [table],
     )
     got = lax.all_to_all(message, "w", 0, 0, tiled=True)
-
-    entry = call(
+    entry, away = call(
         entry_flux_kernel,
         "entry_flux",
-        (place, got, sea, ocean, xc_theta, xc_area, scale),
-        [((Y, NF, OCAP), BF)],
+        (place, got, sea, ocean, theta, area, scale),
+        [((Y, NF, OCAP), BF), ((MSG, RADIUS * CAP), BF)],
     )
     returned = lax.all_to_all(entry, "ocn", 0, 0, tiled=True)
-    back = lax.ppermute(jnp.where(w < W // 2, got[W - RADIUS :], got[:RADIUS]), ("z", "w"), down)
+    back = lax.ppermute(away, ("z", "w"), down)
     atm_flux = call(
         atm_flux_kernel,
         "atm_flux",
-        (place, got, back, air, atm_slots, scale),
+        (place, got, back, air, slot_row, scale),
         [((NF, ATM), F32)],
-    )
-    ocn_flux = call(
-        ocn_flux_kernel, "ocn_flux", (returned, sea_slots), [((NF, OCN), F32)], [index_pad, table], scalar=False
-    )
+        [pltpu.VMEM((W, MSG, CAP), F32)],
+    )
+    ocn_flux = call(ocn_flux_kernel, "ocn_flux", (place, returned, entry_row), [((NF, OCN), F32)], [table])
     return (atm_flux, ocn_flux)
 
 

time: 59.1 us -> 56.4 us (0.954)
  blocking collectives: 0 us -> 10.6 us
  waiting for transfers between devices: 12.9 us -> 6.76 us
  starting transfers between devices: 35.8 us -> 31.2 us
  local copies, waits for them, and re-layouts: 2.93 us -> 0 us
    all_to_all x0 -> x1, blocking collectives: none -> 10.6 us  [on_device(): got = lax.all_to_all(message, 'w', 0, 0, tiled=True)]
    all_to_all x1 -> x0, waiting for transfers between devices: 5.73 us -> none  [on_device(): got = lax.all_to_all(message, 'w', 0, 0, tiled=True)]
    all_to_all x1 -> x0, starting transfers between devices: 4.36 us -> none  [on_device(): got = lax.all_to_all(message, 'w', 0, 0, tiled=True)]
    unnamed x19 -> x0, local copies, waits for them, and re-layouts: 2.84 us -> none
    pallas_call x6 -> x5, Pallas kernels: 6.16 us -> 6.61 us  [call(): pl.pallas_call(kernel, out_shape=shapes[0] if single else shapes, in_spec...]
  transfers between devices with their start and end apart: 5 -> 4, of which waited for: 3 -> 2; matrix products, arithmetic and copies ran while one was open for 0% -> 0% of each run, Pallas kernels for 2% -> 2%
where the time goes in v2:
time: 56.4 us; the launch traced here: 55.9 us
  starting transfers between devices  31.2 us (55%)
  blocking collectives  10.6 us (19%)
  waiting for transfers between devices  6.76 us (12%)
  Pallas kernels  6.61 us (12%)
  between operations  0.67 us (1%)
    all_to_all x1, starting transfers between devices, on_device(): entries = lax.all_to_all(sending, 'ocn', 0, 0, tiled=True)  12.7 us
    all_to_all x1, blocking collectives, on_device(): got = lax.all_to_all(message, 'w', 0, 0, tiled=True)  10.6 us
    ppermute x1, starting transfers between devices, on_device(): crossed = lax.ppermute(cross, ('z', 'w'), up)  9.39 us
    all_to_all x1, starting transfers between devices, on_device(): returned = lax.all_to_all(entry, 'ocn', 0, 0, tiled=True)  7.2 us
    pallas_call x5, Pallas kernels, call(): pl.pallas_call(kernel, out_shape=shapes[0] if single else shapes, in_spec...  6.61 us
    ppermute x1, waiting for transfers between devices, on_device(): back = lax.ppermute(away, ('z', 'w'), down)  5.18 us
    ppermute x1, starting transfers between devices, on_device(): back = lax.ppermute(away, ('z', 'w'), down)  1.91 us
    ppermute x1, waiting for transfers between devices, on_device(): crossed = lax.ppermute(cross, ('z', 'w'), up)  1.58 us
  transfers between devices with their start and end apart: 4, of which 2 were waited for; matrix products, arithmetic and copies ran while one was open for 0% of the time, Pallas kernels for 2%

profile of v2, /device:TPU:8, one launch (start us, length us, event | category | flops | bytes accessed | tf_op | source)
XLA Modules:
  0.0 55.9 jit_solution(2495492328234402510)
XLA Ops:
  0.6 2.4 %send.1 = (bf16[8,64,96]{2,1,0:T(8,128)(2,1)}, bf16[8,64,64]{2,1,0:T(8,128)(2,1)S(1)}, bf16[64,192]{1,0:T(8,128)(2,1)S(1)}, bf16[64,448]{1,0:T(8,128)(2,1)S(1)},...) custom-call(s32[1]{0:T(128)} %bitcast.place_ref, ...), custom_call_target="tpu_custom_call" | custom-call | tf_op jit(solution)/shard_map/send/pallas_call | solution.py:193
  3.0 12.7 %all-to-all-start = ((bf16[8,64,96]{2,1,0:T(8,128)(2,1)}), bf16[8,64,96]{2,1,0:T(8,128)(2,1)S(1)}, u32[]{:S(2)}, u32[]{:S(2)}) async-start(bf16[8,64,96]{2,1,0:T(8,128)(2,1)} %get-tuple-element.16), calls=%async_computation | async-start | bytes 262144 | tf_op jit(solution)/shard_map/all_to_all | solution.py:257
  15.7 9.4 %collective-permute-start = (bf16[64,192]{1,0:T(8,128)(2,1)S(1)}, bf16[64,192]{1,0:T(8,128)(2,1)S(1)}, u32[]{:S(2)}, u32[]{:S(2)}) collective-permute-start(bf16[64,192]{1,0:T(8,128)(2,1)S(1)} %get-tuple-element.21), channel_id=1, source_target_pairs={{0,704},{8,712},{16,720},{40,104},{48,112},{56,120},{64,0},{72,8},... | collective-permute-start | bytes 73736 | tf_op jit(solution)/shard_map/ppermute | solution.py:258
  25.1 1.6 %collective-permute-done.crossed_ref = bf16[64,192]{1,0:T(8,128)(2,1)S(1)} collective-permute-done((bf16[64,192]{1,0:T(8,128)(2,1)S(1)}, bf16[64,192]{1,0:T(8,128)(2,1)S(1)}, u32[]{:S(2)}, u32[]{:S(2)}) %collective-permute-start) | collective-permute-done | bytes 24608 | tf_op jit(solution)/shard_map/ppermute | solution.py:258
  26.7 0.0 all-to-all-done.entries_ref
  26.7 0.6 %make_message.1 = (bf16[64,448]{1,0:T(8,128)(2,1)S(1)}, bf16[8,80,128]{2,1,0:T(8,128)(2,1)S(1)}) custom-call(s32[1]{0:T(128)} %bitcast.place_ref, bf16[8,64,96]{2,1,0:T(8,128)(2,1)S(1)} %all-to-all-done.entries_ref, s32[2,448]{1,0:T(2,128)S(1)} %get-tuple-element.17.ocean_ref, bf16[1,448]{1,0:T(2,128)(2,1)S(1)} %get-tuple-element.18.theta_ref, ...), custom_call_target="tpu_custom_call" | custom-call | tf_op jit(solution)/shard_map/make_message/pallas_call | solution.py:193
  27.3 10.6 %all_to_all.15.got_ref = bf16[8,80,128]{2,1,0:T(8,128)(2,1)S(1)} all-to-all(bf16[8,80,128]{2,1,0:T(8,128)(2,1)S(1)} %get-tuple-element.22), channel_id=1, replica_groups=mesh['z'=12,'w'=8,'ocn'=8] {'w'}, dimensions={0} | all-to-all | bytes 327680 | tf_op jit(solution)/shard_map/all_to_all | solution.py:266
  38.0 1.6 %entry_flux.1 = (bf16[8,64,96]{2,1,0:T(8,128)(2,1)}, bf16[80,192]{1,0:T(8,128)(2,1)S(1)}) custom-call(s32[1]{0:T(128)} %bitcast.place_ref, bf16[8,80,128]{2,1,0:T(8,128)(2,1)S(1)} %all_to_all.15.got_ref, bf16[64,448]{1,0:T(8,128)(2,1)S(1)} %get-tuple-element.23.sea_ref, s32[2,448]{1,0:T(2,128)S(1)} %get-tuple-element.17.ocean_ref, ...), custom_call_target="tpu_custom_call" | custom-call | tf_op jit(solution)/shard_map/entry_flux/pallas_call | solution.py:193
  39.5 7.2 %all-to-all-start.2 = ((bf16[8,64,96]{2,1,0:T(8,128)(2,1)}), bf16[8,64,96]{2,1,0:T(8,128)(2,1)S(1)}, u32[]{:S(2)}, u32[]{:S(2)}) async-start(bf16[8,64,96]{2,1,0:T(8,128)(2,1)} %get-tuple-element.28), calls=%async_computation.2 | async-start | bytes 262144 | tf_op jit(solution)/shard_map/all_to_all | solution.py:273
  46.7 1.9 %collective-permute-start.1 = (bf16[80,192]{1,0:T(8,128)(2,1)S(1)}, bf16[80,192]{1,0:T(8,128)(2,1)S(1)}, u32[]{:S(2)}, u32[]{:S(2)}) collective-permute-start(bf16[80,192]{1,0:T(8,128)(2,1)S(1)} %get-tuple-element.25), channel_id=1, source_target_pairs={{0,64},{8,72},{16,80},{40,744},{48,752},{56,760},{64,128},{72,136}... | collective-permute-start | bytes 92168 | tf_op jit(solution)/shard_map/ppermute | solution.py:274
  48.7 5.2 %collective-permute-done.1.crossed_ref = bf16[80,192]{1,0:T(8,128)(2,1)S(1)} collective-permute-done((bf16[80,192]{1,0:T(8,128)(2,1)S(1)}, bf16[80,192]{1,0:T(8,128)(2,1)S(1)}, u32[]{:S(2)}, u32[]{:S(2)}) %collective-permute-start.1) | collective-permute-done | bytes 30752 | tf_op jit(solution)/shard_map/ppermute | solution.py:274
  53.8 1.1 %atm_flux.1 = f32[64,256]{1,0:T(8,128)} custom-call(s32[1]{0:T(128)} %bitcast.place_ref, bf16[8,80,128]{2,1,0:T(8,128)(2,1)S(1)} %all_to_all.15.got_ref, bf16[80,192]{1,0:T(8,128)(2,1)S(1)} %collective-permute-done.1.crossed_ref, bf16[64,448]{1,0:T(8,128)(2,1)S(1)} %get-tuple-element.26.air_ref, s32[1,448]{1,0:T(1,128)S(1)} %get-tuple-element.27.slots_ref, ...), custom_call_target="tpu_custom_call" | custom-call | tf_op jit(solution)/shard_map/atm_flux/pallas_call | solution.py:193
  54.9 0.0 all-to-all-done.2.returned_ref
  54.9 1.0 %ocn_flux.1 = f32[64,384]{1,0:T(8,128)} custom-call(s32[1]{0:T(128)} %bitcast.place_ref, bf16[8,64,96]{2,1,0:T(8,128)(2,1)S(1)} %all-to-all-done.2.returned_ref, s32[1,1024]{1,0:T(1,128)S(1)} %get-tuple-element.29.entries_ref), custom_call_target="tpu_custom_call" | custom-call | tf_op jit(solution)/shard_map/ocn_flux/pallas_call | solution.py:193
Async XLA Ops:
  3.0 23.7 %all-to-all-start = ((bf16[8,64,96]{2,1,0:T(8,128)(2,1)}), bf16[8,64,96]{2,1,0:T(8,128)(2,1)S(1)}, u32[]{:S(2)}, u32[]{:S(2)}) async-start(bf16[8,64,96]{2,1,0:T(8,128)(2,1)} %get-tuple-element.16), calls=%async_computation | async-start | bytes 262144 | tf_op jit(solution)/shard_map/all_to_all | solution.py:257
  15.7 11.0 %collective-permute-start = (bf16[64,192]{1,0:T(8,128)(2,1)S(1)}, bf16[64,192]{1,0:T(8,128)(2,1)S(1)}, u32[]{:S(2)}, u32[]{:S(2)}) collective-permute-start(bf16[64,192]{1,0:T(8,128)(2,1)S(1)} %get-tuple-element.21), channel_id=1, source_target_pairs={{0,704},{8,712},{16,720},{40,104},{48,112},{56,120},{64,0},{72,8},... | collective-permute-start | bytes 73736 | tf_op jit(solution)/shard_map/ppermute | solution.py:258
  39.5 15.4 %all-to-all-start.2 = ((bf16[8,64,96]{2,1,0:T(8,128)(2,1)}), bf16[8,64,96]{2,1,0:T(8,128)(2,1)S(1)}, u32[]{:S(2)}, u32[]{:S(2)}) async-start(bf16[8,64,96]{2,1,0:T(8,128)(2,1)} %get-tuple-element.28), calls=%async_computation.2 | async-start | bytes 262144 | tf_op jit(solution)/shard_map/all_to_all | solution.py:273
  46.7 7.1 %collective-permute-start.1 = (bf16[80,192]{1,0:T(8,128)(2,1)S(1)}, bf16[80,192]{1,0:T(8,128)(2,1)S(1)}, u32[]{:S(2)}, u32[]{:S(2)}) collective-permute-start(bf16[80,192]{1,0:T(8,128)(2,1)S(1)} %get-tuple-element.25), channel_id=1, source_target_pairs={{0,64},{8,72},{16,80},{40,744},{48,752},{56,760},{64,128},{72,136}... | collective-permute-start | bytes 92168 | tf_op jit(solution)/shard_map/ppermute | solution.py:274

commit v3 on v2

--- a/solution.py
+++ b/solution.py
@@ -20,6 +20,8 @@
 ATM = 256
 OCN = 384
 MSG = NF + 16
+PIECES = 2
+WIDE = 1536
 BF = jnp.bfloat16
 F32 = jnp.float32
 VMEM = pl.BlockSpec(memory_space=pltpu.VMEM)
@@ -59,14 +61,14 @@
 
 
 def summed_onto(values, picker):
-    both = lax.dot_general(halves(values), picker, NT, preferred_element_type=F32)
+    both = lax.dot_general(values, picker, NT, preferred_element_type=F32)
     return both[:NF] + both[NF:]
 
 
 def send_kernel(
     place_ref, ocn_hbm, entries_hbm, atm_hbm, slots_hbm, ocean_hbm, theta_hbm, area_hbm, scale_hbm,
-    out_ref, own_ref, cross_ref, air_ref, entry_row_ref, slot_row_ref, ocean_ref, theta_ref, area_ref, scale_ref,
-    ocn_ref, entries_ref, atm_ref, slots_ref, row_ref, padded, sems,
+    out_hbm, own_ref, cross_ref, wide_ref, air_ref, entry_row_ref, slot_row_ref, ocean_ref, theta_ref, area_ref, scale_ref,
+    ocn_ref, entries_ref, atm_ref, slots_ref, row_ref, padded, placed, out_ref, sems,
 ):
     w = place_ref[0]
     pairs = [
@@ -92,27 +94,34 @@
     picked = jnp.dot(ocn_ref[...], picker, preferred_element_type=F32).astype(BF)
     for o in range(Y):
         out_ref[o] = picked[:, o * PAD : o * PAD + OCAP]
+    leave = pltpu.make_async_copy(out_ref, out_hbm, sems.at[len(pairs)])
+    leave.start()
     copies[2].wait()
-    index = jnp.concatenate([slots_ref[k] for k in range(ROWS)], axis=1)
+    for k in range(ROWS):
+        placed[lax.rem(w + (k - RADIUS + W), W)] = slots_ref[k]
+    placed[lax.rem(w + W // 2, W)] = jnp.full((1, CAP), -1, jnp.int32)
+    index = jnp.concatenate([placed[p] for p in range(W)], axis=1)
     slot_row_ref[...] = index
     picker = one_hot(ATM, index)
     copies[3].wait()
     air = jnp.dot(atm_ref[...], picker, preferred_element_type=F32)
+    crossing = jnp.where(w >= W // 2, air[:, : RADIUS * CAP], air[:, (W - RADIUS) * CAP :]).astype(BF)
+    cross_ref[...] = crossing
+    wide_ref[...] = jnp.zeros((NF, WIDE), BF)
+    wide_ref[:, : RADIUS * CAP] = crossing
     air_ref[...] = air.astype(BF)
-    for k in range(ROWS):
-        own_ref[lax.rem(w + (k - RADIUS + W), W)] = air[:, k * CAP : (k + 1) * CAP].astype(BF)
-    own_ref[lax.rem(w + W // 2, W)] = jnp.zeros((NF, CAP), BF)
-    crossing = [jnp.where(w >= W // 2, own_ref[j], own_ref[W - RADIUS + j]).astype(F32) for j in range(RADIUS)]
-    cross_ref[...] = jnp.concatenate(crossing, axis=1).astype(BF)
+    for p in range(W):
+        own_ref[p] = air[:, p * CAP : (p + 1) * CAP].astype(BF)
     for copy in copies[4:]:
         copy.wait()
     rows = lax.broadcasted_iota(jnp.int32, (NF, NF), 0)
     lanes = lax.broadcasted_iota(jnp.int32, (NF, NF), 1)
     scale_ref[...] = jnp.sum(jnp.where(rows == lanes, row_ref[...], 0.0), axis=1, keepdims=True)
+    leave.wait()
 
 
 def make_message_kernel(
-    place_ref, entries_ref, ocean_ref, theta_ref, area_ref, own_ref, crossed_ref, sea_ref, msg_ref, table
+    place_ref, entries_ref, ocean_ref, theta_ref, area_ref, own_ref, up_ref, down_ref, sea_ref, msg_ref, table
 ):
     w = place_ref[0]
     table[...] = jnp.zeros((NF, EPAD), BF)
@@ -131,7 +140,8 @@
         mine = own_ref[p]
         if p < RADIUS or p >= W - RADIUS:
             j = p if p < RADIUS else p - (W - RADIUS)
-            mine = jnp.where(jnp.abs(p - w) > W // 2, crossed_ref[:, j * CAP : (j + 1) * CAP], mine)
+            there = up_ref if p < RADIUS else down_ref
+            mine = jnp.where(jnp.abs(p - w) > W // 2, there[:, j * CAP : (j + 1) * CAP], mine)
         msg_ref[p, :NF, :CAP] = mine
         msg_ref[p, NF:, :CAP] = jnp.zeros((MSG - NF, CAP), BF)
     for k in range(ROWS):
@@ -140,7 +150,7 @@
 
 
 def entry_flux_kernel(
-    place_ref, got_ref, sea_ref, ocean_ref, theta_ref, area_ref, scale_ref, out_ref, cross_ref
+    place_ref, got_ref, sea_ref, ocean_ref, theta_ref, area_ref, scale_ref, out_hbm, cross_ref, out_ref, sems
 ):
     w = place_ref[0]
     air = jnp.concatenate(
@@ -152,41 +162,76 @@
     )
     index = padded_entries(ocean)
     theta = theta_ref[...].astype(F32)
-    total = summed_onto(theta * weighted, one_hot(EPAD, index[0:1]))
-    total = total + summed_onto((1.0 - theta) * weighted, one_hot(EPAD, index[1:2]))
-    total = total.astype(BF)
-    for o in range(Y):
-        out_ref[o] = total[:, o * PAD : o * PAD + OCAP]
+    one = halves(theta * weighted)
+    two = halves((1.0 - theta) * weighted)
+    part = Y // PIECES
+    copies = []
+    for i in range(PIECES):
+        start = i * part * PAD
+        total = summed_onto(one, one_hot(part * PAD, index[0:1] - start))
+        total = total + summed_onto(two, one_hot(part * PAD, index[1:2] - start))
+        total = total.astype(BF)
+        for o in range(part):
+            out_ref[i * part + o] = total[:, o * PAD : o * PAD + OCAP]
+        rows = pl.ds(i * part, part)
+        copy = pltpu.make_async_copy(out_ref.at[rows], out_hbm.at[rows], sems.at[i])
+        copy.start()
+        copies.append(copy)
     first = jnp.where(w < W // 2, W - RADIUS, 0)
     crossing = [got_ref[first + j, :, CAP:].astype(F32) for j in range(RADIUS)]
     cross_ref[...] = jnp.concatenate(crossing, axis=1).astype(BF)
-
-
-def atm_flux_kernel(place_ref, got_ref, crossed_ref, air_ref, slots_ref, scale_ref, out_ref, spread):
-    w = place_ref[0]
-    for p in range(W):
-        here = got_ref[p, :, CAP:]
-        if p < RADIUS or p >= W - RADIUS:
-            j = p if p < RADIUS else p - (W - RADIUS)
-            here = jnp.where(jnp.abs(p - w) > W // 2, crossed_ref[:, j * CAP : (j + 1) * CAP], here)
-        spread[p] = here.astype(F32)
-    both = jnp.concatenate([spread[lax.rem(w + (k - RADIUS + W), W)] for k in range(ROWS)], axis=1)
-    index = slots_ref[...]
+    for copy in copies:
+        copy.wait()
+
+
+def near_flux_kernel(place_ref, got_ref, air_ref, slots_ref, scale_ref, out_ref):
+    w = place_ref[0]
+    both = jnp.concatenate([got_ref[p, :, CAP:].astype(F32) for p in range(W)], axis=1)
+    slots = slots_ref[...]
+    index = jnp.concatenate(
+        [jnp.where(jnp.abs(p - w) > W // 2, -1, slots[:, p * CAP : (p + 1) * CAP]) for p in range(W)], axis=1
+    )
     weighted = flux(
         air_ref[...].astype(F32), both[:NF], scale_ref[...], both[NF : NF + 1], index >= 0
     )
-    out_ref[...] = summed_onto(weighted, one_hot(ATM, index))
-
-
-def ocn_flux_kernel(place_ref, returned_ref, entries_ref, out_ref, table):
+    out_ref[...] = summed_onto(halves(weighted), one_hot(ATM, index))
+
+
+def last_kernel(
+    place_ref, returned_ref, entries_ref, near_ref, crossed_ref, air_ref, slots_ref, scale_ref,
+    atm_hbm, ocn_hbm, atm_ref, ocn_ref, table, sems,
+):
+    w = place_ref[0]
     table[...] = jnp.zeros((NF, EPAD), BF)
     for o in range(Y):
         table[:, o * PAD : o * PAD + OCAP] = returned_ref[o]
     picker = one_hot(OCN, entries_ref[...])
-    out_ref[...] = lax.dot_general(table[...], picker, NT, preferred_element_type=F32)
-
-
-def call(kernel, name, ins, outs, scratch=(), space=pltpu.VMEM):
+    ocn_ref[...] = lax.dot_general(table[...], picker, NT, preferred_element_type=F32)
+    ocn_copy = pltpu.make_async_copy(ocn_ref, ocn_hbm, sems.at[0])
+    ocn_copy.start()
+    low = w >= W // 2
+    count = RADIUS * CAP
+    last = (W - RADIUS) * CAP
+    air = jnp.where(low, air_ref[:, :count].astype(F32), air_ref[:, last:].astype(F32))
+    slots = jnp.where(low, slots_ref[:, :count], slots_ref[:, last:])
+    first = jnp.where(low, 0, W - RADIUS)
+    index = jnp.concatenate(
+        [
+            jnp.where(jnp.abs(first + j - w) > W // 2, slots[:, j * CAP : (j + 1) * CAP], -1)
+            for j in range(RADIUS)
+        ],
+        axis=1,
+    )
+    both = crossed_ref[...].astype(F32)
+    weighted = flux(air, both[:NF], scale_ref[...], both[NF : NF + 1], index >= 0)
+    atm_ref[...] = near_ref[...] + summed_onto(halves(weighted), one_hot(ATM, index))
+    atm_copy = pltpu.make_async_copy(atm_ref, atm_hbm, sems.at[1])
+    atm_copy.start()
+    ocn_copy.wait()
+    atm_copy.wait()
+
+
+def call(kernel, name, ins, outs, scratch=(), space=pltpu.VMEM, first=pltpu.VMEM, rest=pltpu.VMEM):
     specs = [SMEM] + [pl.BlockSpec(memory_space=space)] * (len(ins) - 1)
     single = len(outs) == 1
     shapes = [jax.ShapeDtypeStruct(s, d) for s, d in outs]
@@ -194,7 +239,7 @@
         kernel,
         out_shape=shapes[0] if single else shapes,
         in_specs=specs,
-        out_specs=VMEM if single else [VMEM] * len(outs),
+        out_specs=pl.BlockSpec(memory_space=first) if single else [pl.BlockSpec(memory_space=x) for x in [first] + [rest] * (len(outs) - 1)],
         scratch_shapes=list(scratch),
         name=name,
         compiler_params=pltpu.CompilerParams(vmem_limit_bytes=24 * 1024 * 1024),
@@ -217,7 +262,7 @@
         xc_area,
         transfer_scale[None, :],
     )
-    sending, own, cross, air, entry_row, slot_row, ocean, theta, area, scale = call(
+    sending, own, cross, wide, air, entry_row, slot_row, ocean, theta, area, scale = call(
         send_kernel,
         "send",
         (place, *(pltpu.with_memory_space_constraint(x, pltpu.HBM) for x in given)),
@@ -225,9 +270,10 @@
             ((Y, NF, OCAP), BF),
             ((W, NF, CAP), BF),
             ((NF, RADIUS * CAP), BF),
-            ((NF, SLOTS), BF),
+            ((NF, WIDE), BF),
+            ((NF, W * CAP), BF),
             ((1, EPAD), jnp.int32),
-            ((1, SLOTS), jnp.int32),
+            ((1, W * CAP), jnp.int32),
             ((2, SLOTS), jnp.int32),
             ((1, SLOTS), BF),
             ((1, SLOTS), BF),
@@ -240,8 +286,11 @@
             pltpu.VMEM((ROWS, 1, CAP), jnp.int32),
             pltpu.VMEM((1, NF), F32),
             pltpu.VMEM((Y, PAD), jnp.int32),
-            pltpu.SemaphoreType.DMA((8,)),
+            pltpu.VMEM((W, 1, CAP), jnp.int32),
+            pltpu.VMEM((Y, NF, OCAP), BF),
+            pltpu.SemaphoreType.DMA((9,)),
         ],
+        pltpu.HBM,
         pltpu.HBM,
     )
     up, down = [], []
@@ -255,11 +304,14 @@
                 up.append((here, below))
                 down.append((here, above))
     entries = lax.all_to_all(sending, "ocn", 0, 0, tiled=True)
-    crossed = lax.ppermute(cross, ("z", "w"), up)
+    rising = [pair for pair in up if pair[0] % W >= W // 2]
+    falling = [pair for pair in up if pair[0] % W < W // 2]
+    crossed_up = lax.ppermute(wide, ("z", "w"), rising)
+    crossed_down = lax.ppermute(cross, ("z", "w"), falling)
     sea, message = call(
         make_message_kernel,
         "make_message",
-        (place, entries, ocean, theta, area, own, crossed),
+        (place, entries, ocean, theta, area, own, crossed_up, crossed_down),
         [((NF, SLOTS), BF), ((W, MSG, 2 * CAP), BF)],
         [table],
     )
@@ -269,18 +321,21 @@
         "entry_flux",
         (place, got, sea, ocean, theta, area, scale),
         [((Y, NF, OCAP), BF), ((MSG, RADIUS * CAP), BF)],
+        [pltpu.VMEM((Y, NF, OCAP), BF), pltpu.SemaphoreType.DMA((PIECES,))],
+        first=pltpu.HBM,
     )
     returned = lax.all_to_all(entry, "ocn", 0, 0, tiled=True)
     back = lax.ppermute(away, ("z", "w"), down)
-    atm_flux = call(
-        atm_flux_kernel,
-        "atm_flux",
-        (place, got, back, air, slot_row, scale),
-        [((NF, ATM), F32)],
-        [pltpu.VMEM((W, MSG, CAP), F32)],
-    )
-    ocn_flux = call(ocn_flux_kernel, "ocn_flux", (place, returned, entry_row), [((NF, OCN), F32)], [table])
-    return (atm_flux, ocn_flux)
+    near = call(near_flux_kernel, "near_flux", (place, got, air, slot_row, scale), [((NF, ATM), F32)])
+    return call(
+        last_kernel,
+        "last",
+        (place, returned, entry_row, near, back, air, slot_row, scale),
+        [((NF, ATM), F32), ((NF, OCN), F32)],
+        [pltpu.VMEM((NF, ATM), F32), pltpu.VMEM((NF, OCN), F32), table, pltpu.SemaphoreType.DMA((2,))],
+        first=pltpu.HBM,
+        rest=pltpu.HBM,
+    )
 
 
 def solution(mesh):

time: 56.4 us -> 55.3 us (0.980)
  blocking collectives: 10.6 us -> 9.05 us
  Pallas kernels: 6.61 us -> 5.55 us
  waiting for transfers between devices: 6.76 us -> 7.59 us
  starting transfers between devices: 31.2 us -> 31.9 us
    all_to_all x1, blocking collectives: 10.6 us -> 9.05 us  [on_device(): got = lax.all_to_all(message, 'w', 0, 0, tiled=True)]
    pallas_call x5, Pallas kernels: 6.61 us -> 5.55 us  [call(): pl.pallas_call(kernel, out_shape=shapes[0] if single else shapes, in_spec...]
    ppermute x1, waiting for transfers between devices: 5.18 us -> 6.01 us  [on_device(): back = lax.ppermute(away, ('z', 'w'), down)]
    ppermute x1 -> x2, starting transfers between devices: 9.39 us -> 10.1 us  [the longest x1 9.39 us: on_device(): crossed_down = lax.ppermute(cross, ('z', 'w'), falling)]
    ppermute x1 -> x2, waiting for transfers between devices: 1.58 us -> 1.58 us  [the longest x1 1.58 us: on_device(): crossed_down = lax.ppermute(cross, ('z', 'w'), falling)]
  transfers between devices with their start and end apart: 4 -> 5, of which waited for: 2 -> 2; matrix products, arithmetic and copies ran while one was open for 0% -> 0% of each run, Pallas kernels for 2% -> 1%
where the time goes in v3:
time: 55.3 us; the launch traced here: 54.8 us
  starting transfers between devices  31.9 us (58%)
  blocking collectives  9.05 us (16%)
  waiting for transfers between devices  7.59 us (14%)
  Pallas kernels  5.55 us (10%)
  between operations  0.7 us (1%)
    all_to_all x1, starting transfers between devices, on_device(): entries = lax.all_to_all(sending, 'ocn', 0, 0, tiled=True)  12.7 us
    ppermute x1, starting transfers between devices, on_device(): crossed_down = lax.ppermute(cross, ('z', 'w'), falling)  9.39 us
    all_to_all x1, blocking collectives, on_device(): got = lax.all_to_all(message, 'w', 0, 0, tiled=True)  9.05 us
    all_to_all x1, starting transfers between devices, on_device(): returned = lax.all_to_all(entry, 'ocn', 0, 0, tiled=True)  7.22 us
    ppermute x1, waiting for transfers between devices, on_device(): back = lax.ppermute(away, ('z', 'w'), down)  6.01 us
    pallas_call x5, Pallas kernels, call(): pl.pallas_call(kernel, out_shape=shapes[0] if single else shapes, in_spec...  5.55 us
    ppermute x1, starting transfers between devices, on_device(): back = lax.ppermute(away, ('z', 'w'), down)  1.91 us
    ppermute x1, waiting for transfers between devices, on_device(): crossed_down = lax.ppermute(cross, ('z', 'w'), falling)  1.58 us
  transfers between devices with their start and end apart: 5, of which 2 were waited for; matrix products, arithmetic and copies ran while one was open for 0% of the time, Pallas kernels for 1%

profile of v3, /device:TPU:8, one launch (start us, length us, event | category | flops | bytes accessed | tf_op | source)
XLA Modules:
  0.0 54.8 jit_solution(5223294897831755831)
XLA Ops:
  0.6 1.9 %send.1 = (bf16[8,64,96]{2,1,0:T(8,128)(2,1)}, bf16[8,64,64]{2,1,0:T(8,128)(2,1)S(1)}, bf16[64,192]{1,0:T(8,128)(2,1)S(1)}, bf16[64,1536]{1,0:T(8,128)(2,1)S(1)}...) custom-call(s32[1]{0:T(128)} %bitcast.place_ref, ...), custom_call_target="tpu_custom_call" | custom-call | tf_op jit(solution)/shard_map/send/pallas_call | solution.py:238
  2.5 0.7 %collective-permute-start = (bf16[64,1536]{1,0:T(8,128)(2,1)S(1)}, bf16[64,1536]{1,0:T(8,128)(2,1)S(1)}, u32[]{:S(2)}, u32[]{:S(2)}) collective-permute-start(bf16[64,1536]{1,0:T(8,128)(2,1)S(1)} %get-tuple-element.22), channel_id=1, source_target_pairs={{40,104},{48,112},{56,120},{104,168},{112,176},{120,184},{168,232}... | collective-permute-start | bytes 589832 | tf_op jit(solution)/shard_map/ppermute | solution.py:309
  3.2 12.7 %all-to-all-start = ((bf16[8,64,96]{2,1,0:T(8,128)(2,1)}), bf16[8,64,96]{2,1,0:T(8,128)(2,1)S(1)}, u32[]{:S(2)}, u32[]{:S(2)}) async-start(bf16[8,64,96]{2,1,0:T(8,128)(2,1)} %get-tuple-element.17), calls=%async_computation | async-start | bytes 262144 | tf_op jit(solution)/shard_map/all_to_all | solution.py:306
  16.0 9.4 %collective-permute-start.1 = (bf16[64,192]{1,0:T(8,128)(2,1)S(1)}, bf16[64,192]{1,0:T(8,128)(2,1)S(1)}, u32[]{:S(2)}, u32[]{:S(2)}) collective-permute-start(bf16[64,192]{1,0:T(8,128)(2,1)S(1)} %get-tuple-element.23), channel_id=1, source_target_pairs={{0,704},{8,712},{16,720},{64,0},{72,8},{80,16},{128,64},{136,72},{... | collective-permute-start | bytes 73736 | tf_op jit(solution)/shard_map/ppermute | solution.py:310
  25.4 1.6 %collective-permute-done.1.down_ref = bf16[64,192]{1,0:T(8,128)(2,1)S(1)} collective-permute-done((bf16[64,192]{1,0:T(8,128)(2,1)S(1)}, bf16[64,192]{1,0:T(8,128)(2,1)S(1)}, u32[]{:S(2)}, u32[]{:S(2)}) %collective-permute-start.1) | collective-permute-done | bytes 24608 | tf_op jit(solution)/shard_map/ppermute | solution.py:310
  26.9 0.0 all-to-all-done.entries_ref
  26.9 0.0 collective-permute-done.up_ref
  26.9 0.6 %make_message.1 = (bf16[64,448]{1,0:T(8,128)(2,1)S(1)}, bf16[8,80,128]{2,1,0:T(8,128)(2,1)S(1)}) custom-call(s32[1]{0:T(128)} %bitcast.place_ref, bf16[8,64,96]{2,1,0:T(8,128)(2,1)S(1)} %all-to-all-done.entries_ref, s32[2,448]{1,0:T(2,128)S(1)} %get-tuple-element.18.ocean_ref, bf16[1,448]{1,0:T(2,128)(2,1)S(1)} %get-tuple-element.19.theta_ref, ...), custom_call_target="tpu_custom_call" | custom-call | tf_op jit(solution)/shard_map/make_message/pallas_call | solution.py:238
  27.5 9.1 %all_to_all.15.got_ref = bf16[8,80,128]{2,1,0:T(8,128)(2,1)S(1)} all-to-all(bf16[8,80,128]{2,1,0:T(8,128)(2,1)S(1)} %get-tuple-element.24), channel_id=1, replica_groups=mesh['z'=12,'w'=8,'ocn'=8] {'w'}, dimensions={0} | all-to-all | bytes 327680 | tf_op jit(solution)/shard_map/all_to_all | solution.py:318
  36.6 1.6 %entry_flux.1 = (bf16[8,64,96]{2,1,0:T(8,128)(2,1)}, bf16[80,192]{1,0:T(8,128)(2,1)S(1)}) custom-call(s32[1]{0:T(128)} %bitcast.place_ref, bf16[8,80,128]{2,1,0:T(8,128)(2,1)S(1)} %all_to_all.15.got_ref, bf16[64,448]{1,0:T(8,128)(2,1)S(1)} %get-tuple-element.25.sea_ref, s32[2,448]{1,0:T(2,128)S(1)} %get-tuple-element.18.ocean_ref, ...), custom_call_target="tpu_custom_call" | custom-call | tf_op jit(solution)/shard_map/entry_flux/pallas_call | solution.py:238
  38.2 7.2 %all-to-all-start.2 = ((bf16[8,64,96]{2,1,0:T(8,128)(2,1)}), bf16[8,64,96]{2,1,0:T(8,128)(2,1)S(1)}, u32[]{:S(2)}, u32[]{:S(2)}) async-start(bf16[8,64,96]{2,1,0:T(8,128)(2,1)} %get-tuple-element.27), calls=%async_computation.2 | async-start | bytes 262144 | tf_op jit(solution)/shard_map/all_to_all | solution.py:327
  45.4 1.9 %collective-permute-start.2 = (bf16[80,192]{1,0:T(8,128)(2,1)S(1)}, bf16[80,192]{1,0:T(8,128)(2,1)S(1)}, u32[]{:S(2)}, u32[]{:S(2)}) collective-permute-start(bf16[80,192]{1,0:T(8,128)(2,1)S(1)} %get-tuple-element.31), channel_id=1, source_target_pairs={{0,64},{8,72},{16,80},{40,744},{48,752},{56,760},{64,128},{72,136}... | collective-permute-start | bytes 92168 | tf_op jit(solution)/shard_map/ppermute | solution.py:328
  47.3 0.4 near_flux.1.near_ref
  47.7 6.0 %collective-permute-done.2.crossed_ref = bf16[80,192]{1,0:T(8,128)(2,1)S(1)} collective-permute-done((bf16[80,192]{1,0:T(8,128)(2,1)S(1)}, bf16[80,192]{1,0:T(8,128)(2,1)S(1)}, u32[]{:S(2)}, u32[]{:S(2)}) %collective-permute-start.2) | collective-permute-done | bytes 30752 | tf_op jit(solution)/shard_map/ppermute | solution.py:328
  53.7 0.0 all-to-all-done.2.returned_ref
  53.7 1.1 %last.1 = (f32[64,256]{1,0:T(8,128)}, f32[64,384]{1,0:T(8,128)}) custom-call(s32[1]{0:T(128)} %bitcast.place_ref, bf16[8,64,96]{2,1,0:T(8,128)(2,1)S(1)} %all-to-all-done.2.returned_ref, s32[1,1024]{1,0:T(1,128)S(1)} %get-tuple-element.28.entries_ref, f32[64,256]{1,0:T(8,128)S(1)} %near_flux.1.near_ref, ...), custom_call_target="tpu_custom_call" | custom-call | tf_op jit(solution)/shard_map/last/pallas_call | solution.py:238
Async XLA Ops:
  2.5 24.4 %collective-permute-start = (bf16[64,1536]{1,0:T(8,128)(2,1)S(1)}, bf16[64,1536]{1,0:T(8,128)(2,1)S(1)}, u32[]{:S(2)}, u32[]{:S(2)}) collective-permute-start(bf16[64,1536]{1,0:T(8,128)(2,1)S(1)} %get-tuple-element.22), channel_id=1, source_target_pairs={{40,104},{48,112},{56,120},{104,168},{112,176},{120,184},{168,232}... | collective-permute-start | bytes 589832 | tf_op jit(solution)/shard_map/ppermute | solution.py:309
  3.2 23.7 %all-to-all-start = ((bf16[8,64,96]{2,1,0:T(8,128)(2,1)}), bf16[8,64,96]{2,1,0:T(8,128)(2,1)S(1)}, u32[]{:S(2)}, u32[]{:S(2)}) async-start(bf16[8,64,96]{2,1,0:T(8,128)(2,1)} %get-tuple-element.17), calls=%async_computation | async-start | bytes 262144 | tf_op jit(solution)/shard_map/all_to_all | solution.py:306
  16.0 11.0 %collective-permute-start.1 = (bf16[64,192]{1,0:T(8,128)(2,1)S(1)}, bf16[64,192]{1,0:T(8,128)(2,1)S(1)}, u32[]{:S(2)}, u32[]{:S(2)}) collective-permute-start(bf16[64,192]{1,0:T(8,128)(2,1)S(1)} %get-tuple-element.23), channel_id=1, source_target_pairs={{0,704},{8,712},{16,720},{64,0},{72,8},{80,16},{128,64},{136,72},{... | collective-permute-start | bytes 73736 | tf_op jit(solution)/shard_map/ppermute | solution.py:310
  38.2 15.5 %all-to-all-start.2 = ((bf16[8,64,96]{2,1,0:T(8,128)(2,1)}), bf16[8,64,96]{2,1,0:T(8,128)(2,1)S(1)}, u32[]{:S(2)}, u32[]{:S(2)}) async-start(bf16[8,64,96]{2,1,0:T(8,128)(2,1)} %get-tuple-element.27), calls=%async_computation.2 | async-start | bytes 262144 | tf_op jit(solution)/shard_map/all_to_all | solution.py:327
  45.4 8.3 %collective-permute-start.2 = (bf16[80,192]{1,0:T(8,128)(2,1)S(1)}, bf16[80,192]{1,0:T(8,128)(2,1)S(1)}, u32[]{:S(2)}, u32[]{:S(2)}) collective-permute-start(bf16[80,192]{1,0:T(8,128)(2,1)S(1)} %get-tuple-element.31), channel_id=1, source_target_pairs={{0,64},{8,72},{16,80},{40,744},{48,752},{56,760},{64,128},{72,136}... | collective-permute-start | bytes 92168 | tf_op jit(solution)/shard_map/ppermute | solution.py:328

commit v4 on v3

--- a/solution.py
+++ b/solution.py
@@ -20,13 +20,11 @@
 ATM = 256
 OCN = 384
 MSG = NF + 16
-PIECES = 2
 WIDE = 1536
 BF = jnp.bfloat16
 F32 = jnp.float32
 VMEM = pl.BlockSpec(memory_space=pltpu.VMEM)
 SMEM = pl.BlockSpec(memory_space=pltpu.SMEM)
-NT = (((1,), (1,)), ((), ()))
 
 
 def one_hot(rows, index):
@@ -60,8 +58,13 @@
     return jnp.concatenate([high, low], axis=0)
 
 
+def one_hot_rows(index, columns):
+    ids = lax.broadcasted_iota(jnp.int32, (index.shape[0], columns), 1)
+    return jnp.where(ids == index, 1.0, 0.0).astype(BF)
+
+
 def summed_onto(values, picker):
-    both = lax.dot_general(values, picker, NT, preferred_element_type=F32)
+    both = jnp.dot(values, picker, preferred_element_type=F32)
     return both[:NF] + both[NF:]
 
 
@@ -120,8 +123,16 @@
     leave.wait()
 
 
+def columns_kernel(place_ref, entries_ref, slots_ref, ocean_ref, out_ref, rows_ref):
+    rows_ref[...] = jnp.full((8, EPAD), -1, jnp.int32)
+    rows_ref[0:1] = entries_ref[...]
+    rows_ref[1:2, : W * CAP] = slots_ref[...]
+    rows_ref[2:4, :SLOTS] = padded_entries(ocean_ref[...])
+    out_ref[...] = rows_ref[...].T
+
+
 def make_message_kernel(
-    place_ref, entries_ref, ocean_ref, theta_ref, area_ref, own_ref, up_ref, down_ref, sea_ref, msg_ref, table
+    place_ref, entries_ref, ocean_ref, theta_ref, area_ref, own_ref, cols_ref, sea_ref, msg_ref, table
 ):
     w = place_ref[0]
     table[...] = jnp.zeros((NF, EPAD), BF)
@@ -137,54 +148,47 @@
     area = jnp.broadcast_to(area_ref[...].astype(F32), (MSG - NF, SLOTS))
     both = jnp.concatenate([sea, area], axis=0)
     for p in range(W):
-        mine = own_ref[p]
-        if p < RADIUS or p >= W - RADIUS:
-            j = p if p < RADIUS else p - (W - RADIUS)
-            there = up_ref if p < RADIUS else down_ref
-            mine = jnp.where(jnp.abs(p - w) > W // 2, there[:, j * CAP : (j + 1) * CAP], mine)
-        msg_ref[p, :NF, :CAP] = mine
+        msg_ref[p, :NF, :CAP] = own_ref[p]
         msg_ref[p, NF:, :CAP] = jnp.zeros((MSG - NF, CAP), BF)
     for k in range(ROWS):
         msg_ref[lax.rem(w + (RADIUS - k + W), W), :, CAP:] = both[:, k * CAP : (k + 1) * CAP].astype(BF)
     msg_ref[lax.rem(w + W // 2, W), :, CAP:] = jnp.zeros((MSG, CAP), BF)
 
 
+def add_crossed_kernel(place_ref, msg_ref, up_ref, down_ref, out_ref):
+    w = place_ref[0]
+    for p in range(W):
+        out_ref[p] = msg_ref[p]
+        if p < RADIUS or p >= W - RADIUS:
+            j = p if p < RADIUS else p - (W - RADIUS)
+            there = up_ref if p < RADIUS else down_ref
+            mine = msg_ref[p, :NF, :CAP]
+            mine = jnp.where(jnp.abs(p - w) > W // 2, there[:, j * CAP : (j + 1) * CAP], mine)
+            out_ref[p, :NF, :CAP] = mine
+
+
 def entry_flux_kernel(
-    place_ref, got_ref, sea_ref, ocean_ref, theta_ref, area_ref, scale_ref, out_hbm, cross_ref, out_ref, sems
+    place_ref, got_ref, sea_ref, ocean_ref, theta_ref, area_ref, scale_ref, cols_ref, out_ref, cross_ref
 ):
     w = place_ref[0]
     air = jnp.concatenate(
         [got_ref[lax.rem(w + (RADIUS - k + W), W), :NF, :CAP].astype(F32) for k in range(ROWS)], axis=1
     )
-    ocean = ocean_ref[...]
     weighted = flux(
-        air, sea_ref[...].astype(F32), scale_ref[...], area_ref[...].astype(F32), ocean[0:1] >= 0
-    )
-    index = padded_entries(ocean)
+        air, sea_ref[...].astype(F32), scale_ref[...], area_ref[...].astype(F32), ocean_ref[0:1, :] >= 0
+    )
     theta = theta_ref[...].astype(F32)
-    one = halves(theta * weighted)
-    two = halves((1.0 - theta) * weighted)
-    part = Y // PIECES
-    copies = []
-    for i in range(PIECES):
-        start = i * part * PAD
-        total = summed_onto(one, one_hot(part * PAD, index[0:1] - start))
-        total = total + summed_onto(two, one_hot(part * PAD, index[1:2] - start))
-        total = total.astype(BF)
-        for o in range(part):
-            out_ref[i * part + o] = total[:, o * PAD : o * PAD + OCAP]
-        rows = pl.ds(i * part, part)
-        copy = pltpu.make_async_copy(out_ref.at[rows], out_hbm.at[rows], sems.at[i])
-        copy.start()
-        copies.append(copy)
+    total = summed_onto(halves(theta * weighted), one_hot_rows(cols_ref[:SLOTS, 2:3], EPAD))
+    total = total + summed_onto(halves((1.0 - theta) * weighted), one_hot_rows(cols_ref[:SLOTS, 3:4], EPAD))
+    total = total.astype(BF)
+    for o in range(Y):
+        out_ref[o] = total[:, o * PAD : o * PAD + OCAP]
     first = jnp.where(w < W // 2, W - RADIUS, 0)
     crossing = [got_ref[first + j, :, CAP:].astype(F32) for j in range(RADIUS)]
     cross_ref[...] = jnp.concatenate(crossing, axis=1).astype(BF)
-    for copy in copies:
-        copy.wait()
-
-
-def near_flux_kernel(place_ref, got_ref, air_ref, slots_ref, scale_ref, out_ref):
+
+
+def near_flux_kernel(place_ref, got_ref, air_ref, slots_ref, scale_ref, cols_ref, out_ref):
     w = place_ref[0]
     both = jnp.concatenate([got_ref[p, :, CAP:].astype(F32) for p in range(W)], axis=1)
     slots = slots_ref[...]
@@ -194,19 +198,21 @@
     weighted = flux(
         air_ref[...].astype(F32), both[:NF], scale_ref[...], both[NF : NF + 1], index >= 0
     )
-    out_ref[...] = summed_onto(halves(weighted), one_hot(ATM, index))
-
-
-def last_kernel(
-    place_ref, returned_ref, entries_ref, near_ref, crossed_ref, air_ref, slots_ref, scale_ref,
-    atm_hbm, ocn_hbm, atm_ref, ocn_ref, table, sems,
-):
-    w = place_ref[0]
+    out_ref[...] = summed_onto(halves(weighted), one_hot_rows(cols_ref[: W * CAP, 1:2], ATM))
+
+
+def ocn_flux_kernel(place_ref, returned_ref, cols_ref, out_ref, table):
     table[...] = jnp.zeros((NF, EPAD), BF)
     for o in range(Y):
         table[:, o * PAD : o * PAD + OCAP] = returned_ref[o]
-    picker = one_hot(OCN, entries_ref[...])
-    ocn_ref[...] = lax.dot_general(table[...], picker, NT, preferred_element_type=F32)
+    out_ref[...] = jnp.dot(table[...], one_hot_rows(cols_ref[:, 0:1], OCN), preferred_element_type=F32)
+
+
+def last_kernel(
+    place_ref, ocn_ref, near_ref, crossed_ref, air_ref, slots_ref, scale_ref, cols_ref,
+    atm_hbm, ocn_hbm, atm_ref, sems,
+):
+    w = place_ref[0]
     ocn_copy = pltpu.make_async_copy(ocn_ref, ocn_hbm, sems.at[0])
     ocn_copy.start()
     low = w >= W // 2
@@ -224,7 +230,8 @@
     )
     both = crossed_ref[...].astype(F32)
     weighted = flux(air, both[:NF], scale_ref[...], both[NF : NF + 1], index >= 0)
-    atm_ref[...] = near_ref[...] + summed_onto(halves(weighted), one_hot(ATM, index))
+    column = jnp.where(low, cols_ref[:count, 1:2], cols_ref[last : last + count, 1:2])
+    atm_ref[...] = near_ref[...] + summed_onto(halves(weighted), one_hot_rows(column, ATM))
     atm_copy = pltpu.make_async_copy(atm_ref, atm_hbm, sems.at[1])
     atm_copy.start()
     ocn_copy.wait()
@@ -293,6 +300,13 @@
         pltpu.HBM,
         pltpu.HBM,
     )
+    cols = call(
+        columns_kernel,
+        "columns",
+        (place, entry_row, slot_row, ocean),
+        [((EPAD, 8), jnp.int32)],
+        [pltpu.VMEM((8, EPAD), jnp.int32)],
+    )
     up, down = [], []
     for z in range(planes):
         for v in range(W):
@@ -311,28 +325,33 @@
     sea, message = call(
         make_message_kernel,
         "make_message",
-        (place, entries, ocean, theta, area, own, crossed_up, crossed_down),
+        (place, entries, ocean, theta, area, own, cols),
         [((NF, SLOTS), BF), ((W, MSG, 2 * CAP), BF)],
         [table],
+    )
+    message = call(
+        add_crossed_kernel,
+        "add_crossed",
+        (place, message, crossed_up, crossed_down),
+        [((W, MSG, 2 * CAP), BF)],
     )
     got = lax.all_to_all(message, "w", 0, 0, tiled=True)
     entry, away = call(
         entry_flux_kernel,
         "entry_flux",
-        (place, got, sea, ocean, theta, area, scale),
+        (place, got, sea, ocean, theta, area, scale, cols),
         [((Y, NF, OCAP), BF), ((MSG, RADIUS * CAP), BF)],
-        [pltpu.VMEM((Y, NF, OCAP), BF), pltpu.SemaphoreType.DMA((PIECES,))],
-        first=pltpu.HBM,
     )
     returned = lax.all_to_all(entry, "ocn", 0, 0, tiled=True)
     back = lax.ppermute(away, ("z", "w"), down)
-    near = call(near_flux_kernel, "near_flux", (place, got, air, slot_row, scale), [((NF, ATM), F32)])
+    near = call(near_flux_kernel, "near_flux", (place, got, air, slot_row, scale, cols), [((NF, ATM), F32)])
+    ocn_flux = call(ocn_flux_kernel, "ocn_flux", (place, returned, cols), [((NF, OCN), F32)], [table])
     return call(
         last_kernel,
         "last",
-        (place, returned, entry_row, near, back, air, slot_row, scale),
+        (place, ocn_flux, near, back, air, slot_row, scale, cols),
         [((NF, ATM), F32), ((NF, OCN), F32)],
-        [pltpu.VMEM((NF, ATM), F32), pltpu.VMEM((NF, OCN), F32), table, pltpu.SemaphoreType.DMA((2,))],
+        [pltpu.VMEM((NF, ATM), F32), pltpu.SemaphoreType.DMA((2,))],
         first=pltpu.HBM,
         rest=pltpu.HBM,
     )

time: 55.3 us -> 55 us (level)
    all_to_all x1, waiting for transfers between devices: 0.01 us -> 5.38 us  [on_device(): returned = lax.all_to_all(entry, 'ocn', 0, 0, tiled=True)]
    ppermute x1, waiting for transfers between devices: 6.01 us -> 0.95 us  [on_device(): back = lax.ppermute(away, ('z', 'w'), down)]
    ppermute x1, waiting for transfers between devices: 1.58 us -> 0.73 us  [on_device(): crossed_down = lax.ppermute(cross, ('z', 'w'), falling)]
    pallas_call x5 -> x8, Pallas kernels: 5.55 us -> 5.75 us  [call(): pl.pallas_call(kernel, out_shape=shapes[0] if single else shapes, in_spec...]
  transfers between devices with their start and end apart: 5 -> 5, of which waited for: 2 -> 3; matrix products, arithmetic and copies ran while one was open for 0% -> 0% of each run, Pallas kernels for 1% -> 3%
where the time goes in v4:
time: 55 us; the launch traced here: 54.5 us
  starting transfers between devices  31.9 us (58%)
  blocking collectives  9.05 us (16%)
  waiting for transfers between devices  7.06 us (13%)
  Pallas kernels  5.75 us (10%)
  between operations  0.71 us (1%)
    all_to_all x1, starting transfers between devices, on_device(): entries = lax.all_to_all(sending, 'ocn', 0, 0, tiled=True)  12.7 us
    ppermute x1, starting transfers between devices, on_device(): crossed_down = lax.ppermute(cross, ('z', 'w'), falling)  9.39 us
    all_to_all x1, blocking collectives, on_device(): got = lax.all_to_all(message, 'w', 0, 0, tiled=True)  9.05 us
    all_to_all x1, starting transfers between devices, on_device(): returned = lax.all_to_all(entry, 'ocn', 0, 0, tiled=True)  7.21 us
    pallas_call x8, Pallas kernels, call(): pl.pallas_call(kernel, out_shape=shapes[0] if single else shapes, in_spec...  5.75 us
    all_to_all x1, waiting for transfers between devices, on_device(): returned = lax.all_to_all(entry, 'ocn', 0, 0, tiled=True)  5.38 us
    ppermute x1, starting transfers between devices, on_device(): back = lax.ppermute(away, ('z', 'w'), down)  1.91 us
  transfers between devices with their start and end apart: 5, of which 3 were waited for; matrix products, arithmetic and copies ran while one was open for 0% of the time, Pallas kernels for 3%

profile of v4, /device:TPU:8, one launch (start us, length us, event | category | flops | bytes accessed | tf_op | source)
XLA Modules:
  0.0 54.5 jit_solution(17003929571869393366)
XLA Ops:
  0.6 1.9 %send.1 = (bf16[8,64,96]{2,1,0:T(8,128)(2,1)}, bf16[8,64,64]{2,1,0:T(8,128)(2,1)S(1)}, bf16[64,192]{1,0:T(8,128)(2,1)S(1)}, bf16[64,1536]{1,0:T(8,128)(2,1)S(1)}...) custom-call(s32[1]{0:T(128)} %bitcast.place_ref, ...), custom_call_target="tpu_custom_call" | custom-call | tf_op jit(solution)/shard_map/send/pallas_call | solution.py:245
  2.5 0.7 %collective-permute-start = (bf16[64,1536]{1,0:T(8,128)(2,1)S(1)}, bf16[64,1536]{1,0:T(8,128)(2,1)S(1)}, u32[]{:S(2)}, u32[]{:S(2)}) collective-permute-start(bf16[64,1536]{1,0:T(8,128)(2,1)S(1)} %get-tuple-element.25), channel_id=1, source_target_pairs={{40,104},{48,112},{56,120},{104,168},{112,176},{120,184},{168,232}... | collective-permute-start | bytes 589832 | tf_op jit(solution)/shard_map/ppermute | solution.py:323
  3.2 12.7 %all-to-all-start = ((bf16[8,64,96]{2,1,0:T(8,128)(2,1)}), bf16[8,64,96]{2,1,0:T(8,128)(2,1)S(1)}, u32[]{:S(2)}, u32[]{:S(2)}) async-start(bf16[8,64,96]{2,1,0:T(8,128)(2,1)} %get-tuple-element.17), calls=%async_computation | async-start | bytes 262144 | tf_op jit(solution)/shard_map/all_to_all | solution.py:320
  16.0 9.4 %collective-permute-start.1 = (bf16[64,192]{1,0:T(8,128)(2,1)S(1)}, bf16[64,192]{1,0:T(8,128)(2,1)S(1)}, u32[]{:S(2)}, u32[]{:S(2)}) collective-permute-start(bf16[64,192]{1,0:T(8,128)(2,1)S(1)} %get-tuple-element.26), channel_id=1, source_target_pairs={{0,704},{8,712},{16,720},{64,0},{72,8},{80,16},{128,64},{136,72},{... | collective-permute-start | bytes 73736 | tf_op jit(solution)/shard_map/ppermute | solution.py:324
  25.4 0.2 columns.1.cols_ref
  25.6 0.0 all-to-all-done.entries_ref
  25.6 0.6 %make_message.1 = (bf16[64,448]{1,0:T(8,128)(2,1)S(1)}, bf16[8,80,128]{2,1,0:T(8,128)(2,1)S(1)}) custom-call(s32[1]{0:T(128)} %bitcast.place_ref, bf16[8,64,96]{2,1,0:T(8,128)(2,1)S(1)} %all-to-all-done.entries_ref, s32[2,448]{1,0:T(2,128)S(1)} %get-tuple-element.18.ocean_ref, bf16[1,448]{1,0:T(2,128)(2,1)S(1)} %get-tuple-element.19.theta_ref, ...), custom_call_target="tpu_custom_call" | custom-call | tf_op jit(solution)/shard_map/make_message/pallas_call | solution.py:245
  26.2 0.7 %collective-permute-done.1.down_ref = bf16[64,192]{1,0:T(8,128)(2,1)S(1)} collective-permute-done((bf16[64,192]{1,0:T(8,128)(2,1)S(1)}, bf16[64,192]{1,0:T(8,128)(2,1)S(1)}, u32[]{:S(2)}, u32[]{:S(2)}) %collective-permute-start.1) | collective-permute-done | bytes 24608 | tf_op jit(solution)/shard_map/ppermute | solution.py:324
  26.9 0.0 collective-permute-done.up_ref
  26.9 0.2 add_crossed.1
  27.1 9.0 %all_to_all.15.got_ref = bf16[8,80,128]{2,1,0:T(8,128)(2,1)S(1)} all-to-all(bf16[8,80,128]{2,1,0:T(8,128)(2,1)S(1)} %add_crossed.1), channel_id=1, replica_groups=mesh['z'=12,'w'=8,'ocn'=8] {'w'}, dimensions={0} | all-to-all | bytes 327680 | tf_op jit(solution)/shard_map/all_to_all | solution.py:338
  36.1 1.3 %entry_flux.1 = (bf16[8,64,96]{2,1,0:T(8,128)(2,1)}, bf16[80,192]{1,0:T(8,128)(2,1)S(1)}) custom-call(s32[1]{0:T(128)} %bitcast.place_ref, bf16[8,80,128]{2,1,0:T(8,128)(2,1)S(1)} %all_to_all.15.got_ref, bf16[64,448]{1,0:T(8,128)(2,1)S(1)} %get-tuple-element.27.sea_ref, s32[2,448]{1,0:T(2,128)S(1)} %get-tuple-element.18.ocean_ref, ...), custom_call_target="tpu_custom_call" | custom-call | tf_op jit(solution)/shard_map/entry_flux/pallas_call | solution.py:245
  37.4 7.2 %all-to-all-start.2 = ((bf16[8,64,96]{2,1,0:T(8,128)(2,1)}), bf16[8,64,96]{2,1,0:T(8,128)(2,1)S(1)}, u32[]{:S(2)}, u32[]{:S(2)}) async-start(bf16[8,64,96]{2,1,0:T(8,128)(2,1)} %get-tuple-element.29), calls=%async_computation.2 | async-start | bytes 262144 | tf_op jit(solution)/shard_map/all_to_all | solution.py:345
  44.6 1.9 %collective-permute-start.2 = (bf16[80,192]{1,0:T(8,128)(2,1)S(1)}, bf16[80,192]{1,0:T(8,128)(2,1)S(1)}, u32[]{:S(2)}, u32[]{:S(2)}) collective-permute-start(bf16[80,192]{1,0:T(8,128)(2,1)S(1)} %get-tuple-element.31), channel_id=1, source_target_pairs={{0,64},{8,72},{16,80},{40,744},{48,752},{56,760},{64,128},{72,136}... | collective-permute-start | bytes 92168 | tf_op jit(solution)/shard_map/ppermute | solution.py:346
  46.5 0.3 near_flux.1.near_ref
  46.9 5.4 %all-to-all-done.2.returned_ref = bf16[8,64,96]{2,1,0:T(8,128)(2,1)S(1)} async-done(((bf16[8,64,96]{2,1,0:T(8,128)(2,1)}), bf16[8,64,96]{2,1,0:T(8,128)(2,1)S(1)}, u32[]{:S(2)}, u32[]{:S(2)}) %all-to-all-start.2) | async-done | bytes 98336 | tf_op jit(solution)/shard_map/all_to_all | solution.py:345
  52.3 0.4 ocn_flux.1.ocn_ref
  52.6 0.9 %collective-permute-done.2.crossed_ref = bf16[80,192]{1,0:T(8,128)(2,1)S(1)} collective-permute-done((bf16[80,192]{1,0:T(8,128)(2,1)S(1)}, bf16[80,192]{1,0:T(8,128)(2,1)S(1)}, u32[]{:S(2)}, u32[]{:S(2)}) %collective-permute-start.2) | collective-permute-done | bytes 30752 | tf_op jit(solution)/shard_map/ppermute | solution.py:346
  53.6 0.9 %last.1 = (f32[64,256]{1,0:T(8,128)}, f32[64,384]{1,0:T(8,128)}) custom-call(s32[1]{0:T(128)} %bitcast.place_ref, f32[64,384]{1,0:T(8,128)S(1)} %ocn_flux.1.ocn_ref, f32[64,256]{1,0:T(8,128)S(1)} %near_flux.1.near_ref, bf16[80,192]{1,0:T(8,128)(2,1)S(1)} %collective-permute-done.2.crossed_ref, bf16[64,512]{1,0:T(8,128)(2,1)S(1)} %get-tuple-element.30.air_ref, ...), custom_call_target="tpu_custom_call" | custom-call | tf_op jit(solution)/shard_map/last/pallas_call | solution.py:245
Async XLA Ops:
  2.5 24.4 %collective-permute-start = (bf16[64,1536]{1,0:T(8,128)(2,1)S(1)}, bf16[64,1536]{1,0:T(8,128)(2,1)S(1)}, u32[]{:S(2)}, u32[]{:S(2)}) collective-permute-start(bf16[64,1536]{1,0:T(8,128)(2,1)S(1)} %get-tuple-element.25), channel_id=1, source_target_pairs={{40,104},{48,112},{56,120},{104,168},{112,176},{120,184},{168,232}... | collective-permute-start | bytes 589832 | tf_op jit(solution)/shard_map/ppermute | solution.py:323
  3.2 22.4 %all-to-all-start = ((bf16[8,64,96]{2,1,0:T(8,128)(2,1)}), bf16[8,64,96]{2,1,0:T(8,128)(2,1)S(1)}, u32[]{:S(2)}, u32[]{:S(2)}) async-start(bf16[8,64,96]{2,1,0:T(8,128)(2,1)} %get-tuple-element.17), calls=%async_computation | async-start | bytes 262144 | tf_op jit(solution)/shard_map/all_to_all | solution.py:320
  16.0 11.0 %collective-permute-start.1 = (bf16[64,192]{1,0:T(8,128)(2,1)S(1)}, bf16[64,192]{1,0:T(8,128)(2,1)S(1)}, u32[]{:S(2)}, u32[]{:S(2)}) collective-permute-start(bf16[64,192]{1,0:T(8,128)(2,1)S(1)} %get-tuple-element.26), channel_id=1, source_target_pairs={{0,704},{8,712},{16,720},{64,0},{72,8},{80,16},{128,64},{136,72},{... | collective-permute-start | bytes 73736 | tf_op jit(solution)/shard_map/ppermute | solution.py:324
  37.4 14.8 %all-to-all-start.2 = ((bf16[8,64,96]{2,1,0:T(8,128)(2,1)}), bf16[8,64,96]{2,1,0:T(8,128)(2,1)S(1)}, u32[]{:S(2)}, u32[]{:S(2)}) async-start(bf16[8,64,96]{2,1,0:T(8,128)(2,1)} %get-tuple-element.29), calls=%async_computation.2 | async-start | bytes 262144 | tf_op jit(solution)/shard_map/all_to_all | solution.py:345
  44.6 8.9 %collective-permute-start.2 = (bf16[80,192]{1,0:T(8,128)(2,1)S(1)}, bf16[80,192]{1,0:T(8,128)(2,1)S(1)}, u32[]{:S(2)}, u32[]{:S(2)}) collective-permute-start(bf16[80,192]{1,0:T(8,128)(2,1)S(1)} %get-tuple-element.31), channel_id=1, source_target_pairs={{0,64},{8,72},{16,80},{40,744},{48,752},{56,760},{64,128},{72,136}... | collective-permute-start | bytes 92168 | tf_op jit(solution)/shard_map/ppermute | solution.py:346

commit v5 on v4

--- a/solution.py
+++ b/solution.py
@@ -19,7 +19,9 @@
 EPAD = Y * PAD
 ATM = 256
 OCN = 384
-MSG = NF + 16
+MSG = NF + 8
+SIDE = PAD - OCAP
+PACK = NF * OCAP // PAD
 WIDE = 1536
 BF = jnp.bfloat16
 F32 = jnp.float32
@@ -37,6 +39,23 @@
     for o in range(1, Y):
         moved = moved + jnp.where(index >= o * OCAP, PAD - OCAP, 0)
     return moved
+
+
+def pack(ref, o, values):
+    ref[o, :, :OCAP] = values[:PACK].astype(BF)
+    beside = [values[PACK:, j * SIDE : (j + 1) * SIDE] for j in range(OCAP // SIDE)]
+    ref[o, :, OCAP:] = jnp.concatenate(beside, axis=0).astype(BF)
+
+
+def unpack(table, ref):
+    table[...] = jnp.zeros((NF, EPAD), BF)
+    for o in range(Y):
+        lanes = slice(o * PAD, o * PAD + OCAP)
+        table[:PACK, lanes] = ref[o, :, :OCAP]
+        beside = ref[o, :, OCAP:].astype(F32)
+        rows = NF - PACK
+        parts = [beside[j * rows : (j + 1) * rows] for j in range(OCAP // SIDE)]
+        table[PACK:, lanes] = jnp.concatenate(parts, axis=1).astype(BF)
 
 
 def flux(air, sea, scale, area, live):
@@ -94,9 +113,9 @@
     entry_row_ref[...] = index
     picker = one_hot(OCN, index)
     copies[1].wait()
-    picked = jnp.dot(ocn_ref[...], picker, preferred_element_type=F32).astype(BF)
+    picked = jnp.dot(ocn_ref[...], picker, preferred_element_type=F32)
     for o in range(Y):
-        out_ref[o] = picked[:, o * PAD : o * PAD + OCAP]
+        pack(out_ref, o, picked[:, o * PAD : o * PAD + OCAP])
     leave = pltpu.make_async_copy(out_ref, out_hbm, sems.at[len(pairs)])
     leave.start()
     copies[2].wait()
@@ -135,9 +154,7 @@
     place_ref, entries_ref, ocean_ref, theta_ref, area_ref, own_ref, cols_ref, sea_ref, msg_ref, table
 ):
     w = place_ref[0]
-    table[...] = jnp.zeros((NF, EPAD), BF)
-    for o in range(Y):
-        table[:, o * PAD : o * PAD + OCAP] = entries_ref[o]
+    unpack(table, entries_ref)
     index = padded_entries(ocean_ref[...])
     entries = table[...]
     first = jnp.dot(entries, one_hot(EPAD, index[0:1]), preferred_element_type=F32)
@@ -148,8 +165,7 @@
     area = jnp.broadcast_to(area_ref[...].astype(F32), (MSG - NF, SLOTS))
     both = jnp.concatenate([sea, area], axis=0)
     for p in range(W):
-        msg_ref[p, :NF, :CAP] = own_ref[p]
-        msg_ref[p, NF:, :CAP] = jnp.zeros((MSG - NF, CAP), BF)
+        msg_ref[p, :, :CAP] = jnp.concatenate([own_ref[p], jnp.zeros((MSG - NF, CAP), BF)], axis=0)
     for k in range(ROWS):
         msg_ref[lax.rem(w + (RADIUS - k + W), W), :, CAP:] = both[:, k * CAP : (k + 1) * CAP].astype(BF)
     msg_ref[lax.rem(w + W // 2, W), :, CAP:] = jnp.zeros((MSG, CAP), BF)
@@ -180,9 +196,8 @@
     theta = theta_ref[...].astype(F32)
     total = summed_onto(halves(theta * weighted), one_hot_rows(cols_ref[:SLOTS, 2:3], EPAD))
     total = total + summed_onto(halves((1.0 - theta) * weighted), one_hot_rows(cols_ref[:SLOTS, 3:4], EPAD))
-    total = total.astype(BF)
     for o in range(Y):
-        out_ref[o] = total[:, o * PAD : o * PAD + OCAP]
+        pack(out_ref, o, total[:, o * PAD : o * PAD + OCAP])
     first = jnp.where(w < W // 2, W - RADIUS, 0)
     crossing = [got_ref[first + j, :, CAP:].astype(F32) for j in range(RADIUS)]
     cross_ref[...] = jnp.concatenate(crossing, axis=1).astype(BF)
@@ -202,9 +217,7 @@
 
 
 def ocn_flux_kernel(place_ref, returned_ref, cols_ref, out_ref, table):
-    table[...] = jnp.zeros((NF, EPAD), BF)
-    for o in range(Y):
-        table[:, o * PAD : o * PAD + OCAP] = returned_ref[o]
+    unpack(table, returned_ref)
     out_ref[...] = jnp.dot(table[...], one_hot_rows(cols_ref[:, 0:1], OCN), preferred_element_type=F32)
 
 
@@ -274,7 +287,7 @@
         "send",
         (place, *(pltpu.with_memory_space_constraint(x, pltpu.HBM) for x in given)),
         [
-            ((Y, NF, OCAP), BF),
+            ((Y, PACK, PAD), BF),
             ((W, NF, CAP), BF),
             ((NF, RADIUS * CAP), BF),
             ((NF, WIDE), BF),
@@ -294,7 +307,7 @@
             pltpu.VMEM((1, NF), F32),
             pltpu.VMEM((Y, PAD), jnp.int32),
             pltpu.VMEM((W, 1, CAP), jnp.int32),
-            pltpu.VMEM((Y, NF, OCAP), BF),
+            pltpu.VMEM((Y, PACK, PAD), BF),
             pltpu.SemaphoreType.DMA((9,)),
         ],
         pltpu.HBM,
@@ -340,7 +353,7 @@
         entry_flux_kernel,
         "entry_flux",
         (place, got, sea, ocean, theta, area, scale, cols),
-        [((Y, NF, OCAP), BF), ((MSG, RADIUS * CAP), BF)],
+        [((Y, PACK, PAD), BF), ((MSG, RADIUS * CAP), BF)],
     )
     returned = lax.all_to_all(entry, "ocn", 0, 0, tiled=True)
     back = lax.ppermute(away, ("z", "w"), down)

time: 55 us -> 54.5 us (level)
  waiting for transfers between devices: 7.06 us -> 6.37 us
where the time goes in v5:
time: 54.5 us; the launch traced here: 54 us
  starting transfers between devices  31.9 us (59%)
  blocking collectives  8.87 us (16%)
  waiting for transfers between devices  6.37 us (12%)
  Pallas kernels  6.15 us (11%)
  between operations  0.71 us (1%)
    all_to_all x1, starting transfers between devices, on_device(): entries = lax.all_to_all(sending, 'ocn', 0, 0, tiled=True)  12.7 us
    ppermute x1, starting transfers between devices, on_device(): crossed_down = lax.ppermute(cross, ('z', 'w'), falling)  9.4 us
    all_to_all x1, blocking collectives, on_device(): got = lax.all_to_all(message, 'w', 0, 0, tiled=True)  8.87 us
    all_to_all x1, starting transfers between devices, on_device(): returned = lax.all_to_all(entry, 'ocn', 0, 0, tiled=True)  7.21 us
    pallas_call x8, Pallas kernels, call(): pl.pallas_call(kernel, out_shape=shapes[0] if single else shapes, in_spec...  6.15 us
    all_to_all x1, waiting for transfers between devices, on_device(): returned = lax.all_to_all(entry, 'ocn', 0, 0, tiled=True)  5.03 us
    ppermute x1, starting transfers between devices, on_device(): back = lax.ppermute(away, ('z', 'w'), down)  1.91 us
  transfers between devices with their start and end apart: 5, of which 3 were waited for; matrix products, arithmetic and copies ran while one was open for 0% of the time, Pallas kernels for 3%

profile of v5, /device:TPU:8, one launch (start us, length us, event | category | flops | bytes accessed | tf_op | source)
XLA Modules:
  0.0 54.0 jit_solution(3955385297483602336)
XLA Ops:
  0.6 2.0 %send.1 = (bf16[8,48,128]{2,1,0:T(8,128)(2,1)}, bf16[8,64,64]{2,1,0:T(8,128)(2,1)S(1)}, bf16[64,192]{1,0:T(8,128)(2,1)S(1)}, bf16[64,1536]{1,0:T(8,128)(2,1)S(1)...) custom-call(s32[1]{0:T(128)} %bitcast.place_ref, ...), custom_call_target="tpu_custom_call" | custom-call | tf_op jit(solution)/shard_map/send/pallas_call | solution.py:258
  2.7 0.7 %collective-permute-start = (bf16[64,1536]{1,0:T(8,128)(2,1)S(1)}, bf16[64,1536]{1,0:T(8,128)(2,1)S(1)}, u32[]{:S(2)}, u32[]{:S(2)}) collective-permute-start(bf16[64,1536]{1,0:T(8,128)(2,1)S(1)} %get-tuple-element.25), channel_id=1, source_target_pairs={{40,104},{48,112},{56,120},{104,168},{112,176},{120,184},{168,232}... | collective-permute-start | bytes 589832 | tf_op jit(solution)/shard_map/ppermute | solution.py:336
  3.4 12.7 %all-to-all-start = ((bf16[8,48,128]{2,1,0:T(8,128)(2,1)}), bf16[8,48,128]{2,1,0:T(8,128)(2,1)S(1)}, u32[]{:S(2)}, u32[]{:S(2)}) async-start(bf16[8,48,128]{2,1,0:T(8,128)(2,1)} %get-tuple-element.17), calls=%async_computation | async-start | bytes 196608 | tf_op jit(solution)/shard_map/all_to_all | solution.py:333
  16.1 9.4 %collective-permute-start.1 = (bf16[64,192]{1,0:T(8,128)(2,1)S(1)}, bf16[64,192]{1,0:T(8,128)(2,1)S(1)}, u32[]{:S(2)}, u32[]{:S(2)}) collective-permute-start(bf16[64,192]{1,0:T(8,128)(2,1)S(1)} %get-tuple-element.26), channel_id=1, source_target_pairs={{0,704},{8,712},{16,720},{64,0},{72,8},{80,16},{128,64},{136,72},{... | collective-permute-start | bytes 73736 | tf_op jit(solution)/shard_map/ppermute | solution.py:337
  25.5 0.2 columns.1.cols_ref
  25.7 0.0 all-to-all-done.entries_ref
  25.7 0.7 %make_message.1 = (bf16[64,448]{1,0:T(8,128)(2,1)S(1)}, bf16[8,72,128]{2,1,0:T(8,128)(2,1)S(1)}) custom-call(s32[1]{0:T(128)} %bitcast.place_ref, bf16[8,48,128]{2,1,0:T(8,128)(2,1)S(1)} %all-to-all-done.entries_ref, s32[2,448]{1,0:T(2,128)S(1)} %get-tuple-element.18.ocean_ref, bf16[1,448]{1,0:T(2,128)(2,1)S(1)} %get-tuple-element.19.theta_ref, ...), custom_call_target="tpu_custom_call" | custom-call | tf_op jit(solution)/shard_map/make_message/pallas_call | solution.py:258
  26.4 0.7 %collective-permute-done.1.down_ref = bf16[64,192]{1,0:T(8,128)(2,1)S(1)} collective-permute-done((bf16[64,192]{1,0:T(8,128)(2,1)S(1)}, bf16[64,192]{1,0:T(8,128)(2,1)S(1)}, u32[]{:S(2)}, u32[]{:S(2)}) %collective-permute-start.1) | collective-permute-done | bytes 24608 | tf_op jit(solution)/shard_map/ppermute | solution.py:337
  27.1 0.0 collective-permute-done.up_ref
  27.1 0.2 add_crossed.1
  27.2 8.9 %all_to_all.15.got_ref = bf16[8,72,128]{2,1,0:T(8,128)(2,1)S(1)} all-to-all(bf16[8,72,128]{2,1,0:T(8,128)(2,1)S(1)} %add_crossed.1), channel_id=1, replica_groups=mesh['z'=12,'w'=8,'ocn'=8] {'w'}, dimensions={0} | all-to-all | bytes 294912 | tf_op jit(solution)/shard_map/all_to_all | solution.py:351
  36.1 1.5 %entry_flux.1 = (bf16[8,48,128]{2,1,0:T(8,128)(2,1)}, bf16[72,192]{1,0:T(8,128)(2,1)S(1)}) custom-call(s32[1]{0:T(128)} %bitcast.place_ref, bf16[8,72,128]{2,1,0:T(8,128)(2,1)S(1)} %all_to_all.15.got_ref, bf16[64,448]{1,0:T(8,128)(2,1)S(1)} %get-tuple-element.27.sea_ref, s32[2,448]{1,0:T(2,128)S(1)} %get-tuple-element.18.ocean_ref, ...), custom_call_target="tpu_custom_call" | custom-call | tf_op jit(solution)/shard_map/entry_flux/pallas_call | solution.py:258
  37.6 7.2 %all-to-all-start.2 = ((bf16[8,48,128]{2,1,0:T(8,128)(2,1)}), bf16[8,48,128]{2,1,0:T(8,128)(2,1)S(1)}, u32[]{:S(2)}, u32[]{:S(2)}) async-start(bf16[8,48,128]{2,1,0:T(8,128)(2,1)} %get-tuple-element.29), calls=%async_computation.2 | async-start | bytes 196608 | tf_op jit(solution)/shard_map/all_to_all | solution.py:358
  44.8 1.9 %collective-permute-start.2 = (bf16[72,192]{1,0:T(8,128)(2,1)S(1)}, bf16[72,192]{1,0:T(8,128)(2,1)S(1)}, u32[]{:S(2)}, u32[]{:S(2)}) collective-permute-start(bf16[72,192]{1,0:T(8,128)(2,1)S(1)} %get-tuple-element.31), channel_id=1, source_target_pairs={{0,64},{8,72},{16,80},{40,744},{48,752},{56,760},{64,128},{72,136}... | collective-permute-start | bytes 82952 | tf_op jit(solution)/shard_map/ppermute | solution.py:359
  46.7 0.3 near_flux.1.near_ref
  47.0 5.0 %all-to-all-done.2.returned_ref = bf16[8,48,128]{2,1,0:T(8,128)(2,1)S(1)} async-done(((bf16[8,48,128]{2,1,0:T(8,128)(2,1)}), bf16[8,48,128]{2,1,0:T(8,128)(2,1)S(1)}, u32[]{:S(2)}, u32[]{:S(2)}) %all-to-all-start.2) | async-done | bytes 98336 | tf_op jit(solution)/shard_map/all_to_all | solution.py:358
  52.0 0.4 ocn_flux.1.ocn_ref
  52.4 0.7 %collective-permute-done.2.crossed_ref = bf16[72,192]{1,0:T(8,128)(2,1)S(1)} collective-permute-done((bf16[72,192]{1,0:T(8,128)(2,1)S(1)}, bf16[72,192]{1,0:T(8,128)(2,1)S(1)}, u32[]{:S(2)}, u32[]{:S(2)}) %collective-permute-start.2) | collective-permute-done | bytes 27680 | tf_op jit(solution)/shard_map/ppermute | solution.py:359
  53.1 0.9 %last.1 = (f32[64,256]{1,0:T(8,128)}, f32[64,384]{1,0:T(8,128)}) custom-call(s32[1]{0:T(128)} %bitcast.place_ref, f32[64,384]{1,0:T(8,128)S(1)} %ocn_flux.1.ocn_ref, f32[64,256]{1,0:T(8,128)S(1)} %near_flux.1.near_ref, bf16[72,192]{1,0:T(8,128)(2,1)S(1)} %collective-permute-done.2.crossed_ref, bf16[64,512]{1,0:T(8,128)(2,1)S(1)} %get-tuple-element.30.air_ref, ...), custom_call_target="tpu_custom_call" | custom-call | tf_op jit(solution)/shard_map/last/pallas_call | solution.py:258
Async XLA Ops:
  2.7 24.4 %collective-permute-start = (bf16[64,1536]{1,0:T(8,128)(2,1)S(1)}, bf16[64,1536]{1,0:T(8,128)(2,1)S(1)}, u32[]{:S(2)}, u32[]{:S(2)}) collective-permute-start(bf16[64,1536]{1,0:T(8,128)(2,1)S(1)} %get-tuple-element.25), channel_id=1, source_target_pairs={{40,104},{48,112},{56,120},{104,168},{112,176},{120,184},{168,232}... | collective-permute-start | bytes 589832 | tf_op jit(solution)/shard_map/ppermute | solution.py:336
  3.4 22.4 %all-to-all-start = ((bf16[8,48,128]{2,1,0:T(8,128)(2,1)}), bf16[8,48,128]{2,1,0:T(8,128)(2,1)S(1)}, u32[]{:S(2)}, u32[]{:S(2)}) async-start(bf16[8,48,128]{2,1,0:T(8,128)(2,1)} %get-tuple-element.17), calls=%async_computation | async-start | bytes 196608 | tf_op jit(solution)/shard_map/all_to_all | solution.py:333
  16.1 11.0 %collective-permute-start.1 = (bf16[64,192]{1,0:T(8,128)(2,1)S(1)}, bf16[64,192]{1,0:T(8,128)(2,1)S(1)}, u32[]{:S(2)}, u32[]{:S(2)}) collective-permute-start(bf16[64,192]{1,0:T(8,128)(2,1)S(1)} %get-tuple-element.26), channel_id=1, source_target_pairs={{0,704},{8,712},{16,720},{64,0},{72,8},{80,16},{128,64},{136,72},{... | collective-permute-start | bytes 73736 | tf_op jit(solution)/shard_map/ppermute | solution.py:337
  37.6 14.5 %all-to-all-start.2 = ((bf16[8,48,128]{2,1,0:T(8,128)(2,1)}), bf16[8,48,128]{2,1,0:T(8,128)(2,1)S(1)}, u32[]{:S(2)}, u32[]{:S(2)}) async-start(bf16[8,48,128]{2,1,0:T(8,128)(2,1)} %get-tuple-element.29), calls=%async_computation.2 | async-start | bytes 196608 | tf_op jit(solution)/shard_map/all_to_all | solution.py:358
  44.8 8.3 %collective-permute-start.2 = (bf16[72,192]{1,0:T(8,128)(2,1)S(1)}, bf16[72,192]{1,0:T(8,128)(2,1)S(1)}, u32[]{:S(2)}, u32[]{:S(2)}) collective-permute-start(bf16[72,192]{1,0:T(8,128)(2,1)S(1)} %get-tuple-element.31), channel_id=1, source_target_pairs={{0,64},{8,72},{16,80},{40,744},{48,752},{56,760},{64,128},{72,136}... | collective-permute-start | bytes 82952 | tf_op jit(solution)/shard_map/ppermute | solution.py:359

commit v6 on v5

--- a/solution.py
+++ b/solution.py
@@ -42,20 +42,23 @@
 
 
 def pack(ref, o, values):
-    ref[o, :, :OCAP] = values[:PACK].astype(BF)
-    beside = [values[PACK:, j * SIDE : (j + 1) * SIDE] for j in range(OCAP // SIDE)]
-    ref[o, :, OCAP:] = jnp.concatenate(beside, axis=0).astype(BF)
+    lanes = lax.broadcasted_iota(jnp.int32, (PACK, PAD), 1)
+    last = values[PACK:]
+    beside = [pltpu.roll(last, OCAP - j * SIDE, 1) for j in range(OCAP // SIDE)]
+    ref[o] = jnp.where(lanes < OCAP, values[:PACK], jnp.concatenate(beside, axis=0)).astype(BF)
 
 
 def unpack(table, ref):
-    table[...] = jnp.zeros((NF, EPAD), BF)
+    rows = NF - PACK
+    lanes = lax.broadcasted_iota(jnp.int32, (rows, PAD), 1)
     for o in range(Y):
-        lanes = slice(o * PAD, o * PAD + OCAP)
-        table[:PACK, lanes] = ref[o, :, :OCAP]
-        beside = ref[o, :, OCAP:].astype(F32)
-        rows = NF - PACK
-        parts = [beside[j * rows : (j + 1) * rows] for j in range(OCAP // SIDE)]
-        table[PACK:, lanes] = jnp.concatenate(parts, axis=1).astype(BF)
+        block = slice(o * PAD, (o + 1) * PAD)
+        table[:PACK, block] = ref[o]
+        last = jnp.zeros((rows, PAD), F32)
+        for j in range(OCAP // SIDE):
+            there = pltpu.roll(ref[o, j * rows : (j + 1) * rows, :].astype(F32), (j + 1) * SIDE, 1)
+            last = jnp.where((lanes >= j * SIDE) & (lanes < (j + 1) * SIDE), there, last)
+        table[PACK:, block] = last.astype(BF)
 
 
 def flux(air, sea, scale, area, live):
@@ -115,7 +118,7 @@
     copies[1].wait()
     picked = jnp.dot(ocn_ref[...], picker, preferred_element_type=F32)
     for o in range(Y):
-        pack(out_ref, o, picked[:, o * PAD : o * PAD + OCAP])
+        pack(out_ref, o, picked[:, o * PAD : (o + 1) * PAD])
     leave = pltpu.make_async_copy(out_ref, out_hbm, sems.at[len(pairs)])
     leave.start()
     copies[2].wait()
@@ -197,7 +200,7 @@
     total = summed_onto(halves(theta * weighted), one_hot_rows(cols_ref[:SLOTS, 2:3], EPAD))
     total = total + summed_onto(halves((1.0 - theta) * weighted), one_hot_rows(cols_ref[:SLOTS, 3:4], EPAD))
     for o in range(Y):
-        pack(out_ref, o, total[:, o * PAD : o * PAD + OCAP])
+        pack(out_ref, o, total[:, o * PAD : (o + 1) * PAD])
     first = jnp.where(w < W // 2, W - RADIUS, 0)
     crossing = [got_ref[first + j, :, CAP:].astype(F32) for j in range(RADIUS)]
     cross_ref[...] = jnp.concatenate(crossing, axis=1).astype(BF)

time: 54.5 us -> 54.3 us (level)
  no operation moved by 1% of the time
where the time goes in v6:
time: 54.3 us; the launch traced here: 53.9 us
  starting transfers between devices  31.9 us (59%)
  blocking collectives  8.87 us (16%)
  waiting for transfers between devices  6.38 us (12%)
  Pallas kernels  5.97 us (11%)
  between operations  0.71 us (1%)
    all_to_all x1, starting transfers between devices, on_device(): entries = lax.all_to_all(sending, 'ocn', 0, 0, tiled=True)  12.7 us
    ppermute x1, starting transfers between devices, on_device(): crossed_down = lax.ppermute(cross, ('z', 'w'), falling)  9.4 us
    all_to_all x1, blocking collectives, on_device(): got = lax.all_to_all(message, 'w', 0, 0, tiled=True)  8.87 us
    all_to_all x1, starting transfers between devices, on_device(): returned = lax.all_to_all(entry, 'ocn', 0, 0, tiled=True)  7.21 us
    pallas_call x8, Pallas kernels, call(): pl.pallas_call(kernel, out_shape=shapes[0] if single else shapes, in_spec...  5.97 us
    all_to_all x1, waiting for transfers between devices, on_device(): returned = lax.all_to_all(entry, 'ocn', 0, 0, tiled=True)  5.03 us
    ppermute x1, starting transfers between devices, on_device(): back = lax.ppermute(away, ('z', 'w'), down)  1.91 us
  transfers between devices with their start and end apart: 5, of which 3 were waited for; matrix products, arithmetic and copies ran while one was open for 0% of the time, Pallas kernels for 3%

profile of v6, /device:TPU:8, one launch (start us, length us, event | category | flops | bytes accessed | tf_op | source)
XLA Modules:
  0.0 53.9 jit_solution(8386459696977234477)
XLA Ops:
  0.6 2.0 %send.1 = (bf16[8,48,128]{2,1,0:T(8,128)(2,1)}, bf16[8,64,64]{2,1,0:T(8,128)(2,1)S(1)}, bf16[64,192]{1,0:T(8,128)(2,1)S(1)}, bf16[64,1536]{1,0:T(8,128)(2,1)S(1)...) custom-call(s32[1]{0:T(128)} %bitcast.place_ref, ...), custom_call_target="tpu_custom_call" | custom-call | tf_op jit(solution)/shard_map/send/pallas_call | solution.py:261
  2.6 0.7 %collective-permute-start = (bf16[64,1536]{1,0:T(8,128)(2,1)S(1)}, bf16[64,1536]{1,0:T(8,128)(2,1)S(1)}, u32[]{:S(2)}, u32[]{:S(2)}) collective-permute-start(bf16[64,1536]{1,0:T(8,128)(2,1)S(1)} %get-tuple-element.25), channel_id=1, source_target_pairs={{40,104},{48,112},{56,120},{104,168},{112,176},{120,184},{168,232}... | collective-permute-start | bytes 589832 | tf_op jit(solution)/shard_map/ppermute | solution.py:339
  3.3 12.7 %all-to-all-start = ((bf16[8,48,128]{2,1,0:T(8,128)(2,1)}), bf16[8,48,128]{2,1,0:T(8,128)(2,1)S(1)}, u32[]{:S(2)}, u32[]{:S(2)}) async-start(bf16[8,48,128]{2,1,0:T(8,128)(2,1)} %get-tuple-element.17), calls=%async_computation | async-start | bytes 196608 | tf_op jit(solution)/shard_map/all_to_all | solution.py:336
  16.0 9.4 %collective-permute-start.1 = (bf16[64,192]{1,0:T(8,128)(2,1)S(1)}, bf16[64,192]{1,0:T(8,128)(2,1)S(1)}, u32[]{:S(2)}, u32[]{:S(2)}) collective-permute-start(bf16[64,192]{1,0:T(8,128)(2,1)S(1)} %get-tuple-element.26), channel_id=1, source_target_pairs={{0,704},{8,712},{16,720},{64,0},{72,8},{80,16},{128,64},{136,72},{... | collective-permute-start | bytes 73736 | tf_op jit(solution)/shard_map/ppermute | solution.py:340
  25.4 0.2 columns.1.cols_ref
  25.7 0.0 all-to-all-done.entries_ref
  25.7 0.7 %make_message.1 = (bf16[64,448]{1,0:T(8,128)(2,1)S(1)}, bf16[8,72,128]{2,1,0:T(8,128)(2,1)S(1)}) custom-call(s32[1]{0:T(128)} %bitcast.place_ref, bf16[8,48,128]{2,1,0:T(8,128)(2,1)S(1)} %all-to-all-done.entries_ref, s32[2,448]{1,0:T(2,128)S(1)} %get-tuple-element.18.ocean_ref, bf16[1,448]{1,0:T(2,128)(2,1)S(1)} %get-tuple-element.19.theta_ref, ...), custom_call_target="tpu_custom_call" | custom-call | tf_op jit(solution)/shard_map/make_message/pallas_call | solution.py:261
  26.3 0.7 %collective-permute-done.1.down_ref = bf16[64,192]{1,0:T(8,128)(2,1)S(1)} collective-permute-done((bf16[64,192]{1,0:T(8,128)(2,1)S(1)}, bf16[64,192]{1,0:T(8,128)(2,1)S(1)}, u32[]{:S(2)}, u32[]{:S(2)}) %collective-permute-start.1) | collective-permute-done | bytes 24608 | tf_op jit(solution)/shard_map/ppermute | solution.py:340
  27.0 0.0 collective-permute-done.up_ref
  27.0 0.2 add_crossed.1
  27.2 8.9 %all_to_all.15.got_ref = bf16[8,72,128]{2,1,0:T(8,128)(2,1)S(1)} all-to-all(bf16[8,72,128]{2,1,0:T(8,128)(2,1)S(1)} %add_crossed.1), channel_id=1, replica_groups=mesh['z'=12,'w'=8,'ocn'=8] {'w'}, dimensions={0} | all-to-all | bytes 294912 | tf_op jit(solution)/shard_map/all_to_all | solution.py:354
  36.0 1.4 %entry_flux.1 = (bf16[8,48,128]{2,1,0:T(8,128)(2,1)}, bf16[72,192]{1,0:T(8,128)(2,1)S(1)}) custom-call(s32[1]{0:T(128)} %bitcast.place_ref, bf16[8,72,128]{2,1,0:T(8,128)(2,1)S(1)} %all_to_all.15.got_ref, bf16[64,448]{1,0:T(8,128)(2,1)S(1)} %get-tuple-element.27.sea_ref, s32[2,448]{1,0:T(2,128)S(1)} %get-tuple-element.18.ocean_ref, ...), custom_call_target="tpu_custom_call" | custom-call | tf_op jit(solution)/shard_map/entry_flux/pallas_call | solution.py:261
  37.4 7.2 %all-to-all-start.2 = ((bf16[8,48,128]{2,1,0:T(8,128)(2,1)}), bf16[8,48,128]{2,1,0:T(8,128)(2,1)S(1)}, u32[]{:S(2)}, u32[]{:S(2)}) async-start(bf16[8,48,128]{2,1,0:T(8,128)(2,1)} %get-tuple-element.29), calls=%async_computation.2 | async-start | bytes 196608 | tf_op jit(solution)/shard_map/all_to_all | solution.py:361
  44.6 1.9 %collective-permute-start.2 = (bf16[72,192]{1,0:T(8,128)(2,1)S(1)}, bf16[72,192]{1,0:T(8,128)(2,1)S(1)}, u32[]{:S(2)}, u32[]{:S(2)}) collective-permute-start(bf16[72,192]{1,0:T(8,128)(2,1)S(1)} %get-tuple-element.31), channel_id=1, source_target_pairs={{0,64},{8,72},{16,80},{40,744},{48,752},{56,760},{64,128},{72,136}... | collective-permute-start | bytes 82952 | tf_op jit(solution)/shard_map/ppermute | solution.py:362
  46.5 0.3 near_flux.1.near_ref
  46.8 5.0 %all-to-all-done.2.returned_ref = bf16[8,48,128]{2,1,0:T(8,128)(2,1)S(1)} async-done(((bf16[8,48,128]{2,1,0:T(8,128)(2,1)}), bf16[8,48,128]{2,1,0:T(8,128)(2,1)S(1)}, u32[]{:S(2)}, u32[]{:S(2)}) %all-to-all-start.2) | async-done | bytes 98336 | tf_op jit(solution)/shard_map/all_to_all | solution.py:361
  51.9 0.4 ocn_flux.1.ocn_ref
  52.3 0.7 %collective-permute-done.2.crossed_ref = bf16[72,192]{1,0:T(8,128)(2,1)S(1)} collective-permute-done((bf16[72,192]{1,0:T(8,128)(2,1)S(1)}, bf16[72,192]{1,0:T(8,128)(2,1)S(1)}, u32[]{:S(2)}, u32[]{:S(2)}) %collective-permute-start.2) | collective-permute-done | bytes 27680 | tf_op jit(solution)/shard_map/ppermute | solution.py:362
  52.9 0.9 %last.1 = (f32[64,256]{1,0:T(8,128)}, f32[64,384]{1,0:T(8,128)}) custom-call(s32[1]{0:T(128)} %bitcast.place_ref, f32[64,384]{1,0:T(8,128)S(1)} %ocn_flux.1.ocn_ref, f32[64,256]{1,0:T(8,128)S(1)} %near_flux.1.near_ref, bf16[72,192]{1,0:T(8,128)(2,1)S(1)} %collective-permute-done.2.crossed_ref, bf16[64,512]{1,0:T(8,128)(2,1)S(1)} %get-tuple-element.30.air_ref, ...), custom_call_target="tpu_custom_call" | custom-call | tf_op jit(solution)/shard_map/last/pallas_call | solution.py:261
Async XLA Ops:
  2.6 24.4 %collective-permute-start = (bf16[64,1536]{1,0:T(8,128)(2,1)S(1)}, bf16[64,1536]{1,0:T(8,128)(2,1)S(1)}, u32[]{:S(2)}, u32[]{:S(2)}) collective-permute-start(bf16[64,1536]{1,0:T(8,128)(2,1)S(1)} %get-tuple-element.25), channel_id=1, source_target_pairs={{40,104},{48,112},{56,120},{104,168},{112,176},{120,184},{168,232}... | collective-permute-start | bytes 589832 | tf_op jit(solution)/shard_map/ppermute | solution.py:339
  3.3 22.4 %all-to-all-start = ((bf16[8,48,128]{2,1,0:T(8,128)(2,1)}), bf16[8,48,128]{2,1,0:T(8,128)(2,1)S(1)}, u32[]{:S(2)}, u32[]{:S(2)}) async-start(bf16[8,48,128]{2,1,0:T(8,128)(2,1)} %get-tuple-element.17), calls=%async_computation | async-start | bytes 196608 | tf_op jit(solution)/shard_map/all_to_all | solution.py:336
  16.0 11.0 %collective-permute-start.1 = (bf16[64,192]{1,0:T(8,128)(2,1)S(1)}, bf16[64,192]{1,0:T(8,128)(2,1)S(1)}, u32[]{:S(2)}, u32[]{:S(2)}) collective-permute-start(bf16[64,192]{1,0:T(8,128)(2,1)S(1)} %get-tuple-element.26), channel_id=1, source_target_pairs={{0,704},{8,712},{16,720},{64,0},{72,8},{80,16},{128,64},{136,72},{... | collective-permute-start | bytes 73736 | tf_op jit(solution)/shard_map/ppermute | solution.py:340
  37.4 14.5 %all-to-all-start.2 = ((bf16[8,48,128]{2,1,0:T(8,128)(2,1)}), bf16[8,48,128]{2,1,0:T(8,128)(2,1)S(1)}, u32[]{:S(2)}, u32[]{:S(2)}) async-start(bf16[8,48,128]{2,1,0:T(8,128)(2,1)} %get-tuple-element.29), calls=%async_computation.2 | async-start | bytes 196608 | tf_op jit(solution)/shard_map/all_to_all | solution.py:361
  44.6 8.3 %collective-permute-start.2 = (bf16[72,192]{1,0:T(8,128)(2,1)S(1)}, bf16[72,192]{1,0:T(8,128)(2,1)S(1)}, u32[]{:S(2)}, u32[]{:S(2)}) collective-permute-start(bf16[72,192]{1,0:T(8,128)(2,1)S(1)} %get-tuple-element.31), channel_id=1, source_target_pairs={{0,64},{8,72},{16,80},{40,744},{48,752},{56,760},{64,128},{72,136}... | collective-permute-start | bytes 82952 | tf_op jit(solution)/shard_map/ppermute | solution.py:362

commit v7 on v6

--- a/solution.py
+++ b/solution.py
@@ -22,7 +22,7 @@
 MSG = NF + 8
 SIDE = PAD - OCAP
 PACK = NF * OCAP // PAD
-WIDE = 1536
+WIDE = 1408
 BF = jnp.bfloat16
 F32 = jnp.float32
 VMEM = pl.BlockSpec(memory_space=pltpu.VMEM)

time: 54.3 us -> 54.3 us (level)
  no operation moved by 1% of the time
where the time goes in v7:
time: 54.3 us; the launch traced here: 53.8 us
  starting transfers between devices  31.9 us (59%)
  blocking collectives  8.86 us (16%)
  waiting for transfers between devices  6.37 us (12%)
  Pallas kernels  5.97 us (11%)
  between operations  0.71 us (1%)
    all_to_all x1, starting transfers between devices, on_device(): entries = lax.all_to_all(sending, 'ocn', 0, 0, tiled=True)  12.7 us
    ppermute x1, starting transfers between devices, on_device(): crossed_down = lax.ppermute(cross, ('z', 'w'), falling)  9.4 us
    all_to_all x1, blocking collectives, on_device(): got = lax.all_to_all(message, 'w', 0, 0, tiled=True)  8.86 us
    all_to_all x1, starting transfers between devices, on_device(): returned = lax.all_to_all(entry, 'ocn', 0, 0, tiled=True)  7.21 us
    pallas_call x8, Pallas kernels, call(): pl.pallas_call(kernel, out_shape=shapes[0] if single else shapes, in_spec...  5.97 us
    all_to_all x1, waiting for transfers between devices, on_device(): returned = lax.all_to_all(entry, 'ocn', 0, 0, tiled=True)  5.03 us
    ppermute x1, starting transfers between devices, on_device(): back = lax.ppermute(away, ('z', 'w'), down)  1.91 us
  transfers between devices with their start and end apart: 5, of which 3 were waited for; matrix products, arithmetic and copies ran while one was open for 0% of the time, Pallas kernels for 3%

profile of v7, /device:TPU:8, one launch (start us, length us, event | category | flops | bytes accessed | tf_op | source)
XLA Modules:
  0.0 53.8 jit_solution(81699182701593204)
XLA Ops:
  0.6 2.0 %send.1 = (bf16[8,48,128]{2,1,0:T(8,128)(2,1)}, bf16[8,64,64]{2,1,0:T(8,128)(2,1)S(1)}, bf16[64,192]{1,0:T(8,128)(2,1)S(1)}, bf16[64,1408]{1,0:T(8,128)(2,1)S(1)...) custom-call(s32[1]{0:T(128)} %bitcast.place_ref, ...), custom_call_target="tpu_custom_call" | custom-call | tf_op jit(solution)/shard_map/send/pallas_call | solution.py:261
  2.6 0.7 %collective-permute-start = (bf16[64,1408]{1,0:T(8,128)(2,1)S(1)}, bf16[64,1408]{1,0:T(8,128)(2,1)S(1)}, u32[]{:S(2)}, u32[]{:S(2)}) collective-permute-start(bf16[64,1408]{1,0:T(8,128)(2,1)S(1)} %get-tuple-element.25), channel_id=1, source_target_pairs={{40,104},{48,112},{56,120},{104,168},{112,176},{120,184},{168,232}... | collective-permute-start | bytes 540680 | tf_op jit(solution)/shard_map/ppermute | solution.py:339
  3.3 12.7 %all-to-all-start = ((bf16[8,48,128]{2,1,0:T(8,128)(2,1)}), bf16[8,48,128]{2,1,0:T(8,128)(2,1)S(1)}, u32[]{:S(2)}, u32[]{:S(2)}) async-start(bf16[8,48,128]{2,1,0:T(8,128)(2,1)} %get-tuple-element.17), calls=%async_computation | async-start | bytes 196608 | tf_op jit(solution)/shard_map/all_to_all | solution.py:336
  16.0 9.4 %collective-permute-start.1 = (bf16[64,192]{1,0:T(8,128)(2,1)S(1)}, bf16[64,192]{1,0:T(8,128)(2,1)S(1)}, u32[]{:S(2)}, u32[]{:S(2)}) collective-permute-start(bf16[64,192]{1,0:T(8,128)(2,1)S(1)} %get-tuple-element.26), channel_id=1, source_target_pairs={{0,704},{8,712},{16,720},{64,0},{72,8},{80,16},{128,64},{136,72},{... | collective-permute-start | bytes 73736 | tf_op jit(solution)/shard_map/ppermute | solution.py:340
  25.4 0.2 columns.1.cols_ref
  25.7 0.0 all-to-all-done.entries_ref
  25.7 0.7 %make_message.1 = (bf16[64,448]{1,0:T(8,128)(2,1)S(1)}, bf16[8,72,128]{2,1,0:T(8,128)(2,1)S(1)}) custom-call(s32[1]{0:T(128)} %bitcast.place_ref, bf16[8,48,128]{2,1,0:T(8,128)(2,1)S(1)} %all-to-all-done.entries_ref, s32[2,448]{1,0:T(2,128)S(1)} %get-tuple-element.18.ocean_ref, bf16[1,448]{1,0:T(2,128)(2,1)S(1)} %get-tuple-element.19.theta_ref, ...), custom_call_target="tpu_custom_call" | custom-call | tf_op jit(solution)/shard_map/make_message/pallas_call | solution.py:261
  26.3 0.7 %collective-permute-done.1.down_ref = bf16[64,192]{1,0:T(8,128)(2,1)S(1)} collective-permute-done((bf16[64,192]{1,0:T(8,128)(2,1)S(1)}, bf16[64,192]{1,0:T(8,128)(2,1)S(1)}, u32[]{:S(2)}, u32[]{:S(2)}) %collective-permute-start.1) | collective-permute-done | bytes 24608 | tf_op jit(solution)/shard_map/ppermute | solution.py:340
  27.0 0.0 collective-permute-done.up_ref
  27.0 0.2 add_crossed.1
  27.2 8.9 %all_to_all.15.got_ref = bf16[8,72,128]{2,1,0:T(8,128)(2,1)S(1)} all-to-all(bf16[8,72,128]{2,1,0:T(8,128)(2,1)S(1)} %add_crossed.1), channel_id=1, replica_groups=mesh['z'=12,'w'=8,'ocn'=8] {'w'}, dimensions={0} | all-to-all | bytes 294912 | tf_op jit(solution)/shard_map/all_to_all | solution.py:354
  36.0 1.4 %entry_flux.1 = (bf16[8,48,128]{2,1,0:T(8,128)(2,1)}, bf16[72,192]{1,0:T(8,128)(2,1)S(1)}) custom-call(s32[1]{0:T(128)} %bitcast.place_ref, bf16[8,72,128]{2,1,0:T(8,128)(2,1)S(1)} %all_to_all.15.got_ref, bf16[64,448]{1,0:T(8,128)(2,1)S(1)} %get-tuple-element.27.sea_ref, s32[2,448]{1,0:T(2,128)S(1)} %get-tuple-element.18.ocean_ref, ...), custom_call_target="tpu_custom_call" | custom-call | tf_op jit(solution)/shard_map/entry_flux/pallas_call | solution.py:261
  37.4 7.2 %all-to-all-start.2 = ((bf16[8,48,128]{2,1,0:T(8,128)(2,1)}), bf16[8,48,128]{2,1,0:T(8,128)(2,1)S(1)}, u32[]{:S(2)}, u32[]{:S(2)}) async-start(bf16[8,48,128]{2,1,0:T(8,128)(2,1)} %get-tuple-element.29), calls=%async_computation.2 | async-start | bytes 196608 | tf_op jit(solution)/shard_map/all_to_all | solution.py:361
  44.6 1.9 %collective-permute-start.2 = (bf16[72,192]{1,0:T(8,128)(2,1)S(1)}, bf16[72,192]{1,0:T(8,128)(2,1)S(1)}, u32[]{:S(2)}, u32[]{:S(2)}) collective-permute-start(bf16[72,192]{1,0:T(8,128)(2,1)S(1)} %get-tuple-element.31), channel_id=1, source_target_pairs={{0,64},{8,72},{16,80},{40,744},{48,752},{56,760},{64,128},{72,136}... | collective-permute-start | bytes 82952 | tf_op jit(solution)/shard_map/ppermute | solution.py:362
  46.5 0.3 near_flux.1.near_ref
  46.8 5.0 %all-to-all-done.2.returned_ref = bf16[8,48,128]{2,1,0:T(8,128)(2,1)S(1)} async-done(((bf16[8,48,128]{2,1,0:T(8,128)(2,1)}), bf16[8,48,128]{2,1,0:T(8,128)(2,1)S(1)}, u32[]{:S(2)}, u32[]{:S(2)}) %all-to-all-start.2) | async-done | bytes 98336 | tf_op jit(solution)/shard_map/all_to_all | solution.py:361
  51.9 0.4 ocn_flux.1.ocn_ref
  52.2 0.7 %collective-permute-done.2.crossed_ref = bf16[72,192]{1,0:T(8,128)(2,1)S(1)} collective-permute-done((bf16[72,192]{1,0:T(8,128)(2,1)S(1)}, bf16[72,192]{1,0:T(8,128)(2,1)S(1)}, u32[]{:S(2)}, u32[]{:S(2)}) %collective-permute-start.2) | collective-permute-done | bytes 27680 | tf_op jit(solution)/shard_map/ppermute | solution.py:362
  52.9 0.9 %last.1 = (f32[64,256]{1,0:T(8,128)}, f32[64,384]{1,0:T(8,128)}) custom-call(s32[1]{0:T(128)} %bitcast.place_ref, f32[64,384]{1,0:T(8,128)S(1)} %ocn_flux.1.ocn_ref, f32[64,256]{1,0:T(8,128)S(1)} %near_flux.1.near_ref, bf16[72,192]{1,0:T(8,128)(2,1)S(1)} %collective-permute-done.2.crossed_ref, bf16[64,512]{1,0:T(8,128)(2,1)S(1)} %get-tuple-element.30.air_ref, ...), custom_call_target="tpu_custom_call" | custom-call | tf_op jit(solution)/shard_map/last/pallas_call | solution.py:261
Async XLA Ops:
  2.6 24.4 %collective-permute-start = (bf16[64,1408]{1,0:T(8,128)(2,1)S(1)}, bf16[64,1408]{1,0:T(8,128)(2,1)S(1)}, u32[]{:S(2)}, u32[]{:S(2)}) collective-permute-start(bf16[64,1408]{1,0:T(8,128)(2,1)S(1)} %get-tuple-element.25), channel_id=1, source_target_pairs={{40,104},{48,112},{56,120},{104,168},{112,176},{120,184},{168,232}... | collective-permute-start | bytes 540680 | tf_op jit(solution)/shard_map/ppermute | solution.py:339
  3.3 22.4 %all-to-all-start = ((bf16[8,48,128]{2,1,0:T(8,128)(2,1)}), bf16[8,48,128]{2,1,0:T(8,128)(2,1)S(1)}, u32[]{:S(2)}, u32[]{:S(2)}) async-start(bf16[8,48,128]{2,1,0:T(8,128)(2,1)} %get-tuple-element.17), calls=%async_computation | async-start | bytes 196608 | tf_op jit(solution)/shard_map/all_to_all | solution.py:336
  16.0 11.0 %collective-permute-start.1 = (bf16[64,192]{1,0:T(8,128)(2,1)S(1)}, bf16[64,192]{1,0:T(8,128)(2,1)S(1)}, u32[]{:S(2)}, u32[]{:S(2)}) collective-permute-start(bf16[64,192]{1,0:T(8,128)(2,1)S(1)} %get-tuple-element.26), channel_id=1, source_target_pairs={{0,704},{8,712},{16,720},{64,0},{72,8},{80,16},{128,64},{136,72},{... | collective-permute-start | bytes 73736 | tf_op jit(solution)/shard_map/ppermute | solution.py:340
  37.4 14.5 %all-to-all-start.2 = ((bf16[8,48,128]{2,1,0:T(8,128)(2,1)}), bf16[8,48,128]{2,1,0:T(8,128)(2,1)S(1)}, u32[]{:S(2)}, u32[]{:S(2)}) async-start(bf16[8,48,128]{2,1,0:T(8,128)(2,1)} %get-tuple-element.29), calls=%async_computation.2 | async-start | bytes 196608 | tf_op jit(solution)/shard_map/all_to_all | solution.py:361
  44.6 8.3 %collective-permute-start.2 = (bf16[72,192]{1,0:T(8,128)(2,1)S(1)}, bf16[72,192]{1,0:T(8,128)(2,1)S(1)}, u32[]{:S(2)}, u32[]{:S(2)}) collective-permute-start(bf16[72,192]{1,0:T(8,128)(2,1)S(1)} %get-tuple-element.31), channel_id=1, source_target_pairs={{0,64},{8,72},{16,80},{40,744},{48,752},{56,760},{64,128},{72,136}... | collective-permute-start | bytes 82952 | tf_op jit(solution)/shard_map/ppermute | solution.py:362
